TPU v7x, 256 devices: a whole 4x4x8 slice. The times are simulated.
256 devices in a mesh: pair: 8 (over x, core), elem: 32 (over z, y).
Axes of the slice: x: 4, y: 4, z: 8, core: 2. Of those that a mesh axis runs over, the one named last changes fastest.
Arguments:
- gas_amounts: float32 [7, 24, 524288], P(None, None, ('pair', 'elem')), may hold values from 0.01 to 0.1
- layer_mass: float32 [24, 524288], P(None, ('pair', 'elem')), may hold values from 0.5 to 1.5
- cloud_paths: float32 [2, 24, 524288], P(None, None, ('pair', 'elem')), may hold values from 0 to 0.3
- surface_kind: int32 [524288], P(('pair', 'elem')), may hold values from 0 to 3
- snow_cover: float32 [524288], P(('pair', 'elem')), may hold values from 0 to 1
- snow_age: float32 [524288], P(('pair', 'elem')), may hold values from 0 to 1
- cos_zenith: float32 [524288], P(('pair', 'elem')), may hold values from 0.05 to 1
- sunlit: int32 [524288], P(('pair', 'elem')), may hold values from 0 to 1, as said below
- gas_coeff: float32 [7, 112], replicated, may hold values from 0.001 to 3
- rayleigh: float32 [112], replicated, may hold values from 0.001 to 0.05
- cloud_ext: float32 [2, 14], replicated, may hold values from 0.5 to 5
- surface_table: float32 [4, 14], replicated, may hold values from 0.03 to 0.6
- snow_table: float32 [14], replicated, may hold values from 0.5 to 0.95
- solar_weight: float32 [112], replicated, may hold values from 0.1 to 1
Outputs:
- heating: float32 [24, 524288], P(None, ('pair', 'elem'))
- surface_net: float32 [524288], P(('pair', 'elem'))
Inputs may be any that keep to these rules, and one draw needn't show every extreme that they name: The columns at physics positions i and i + 262144 are never both sunlit.
All inputs are finite; a program needn't handle non-finite values.
Results may differ from a plain program's by a relative error of at most 0.0001.
Values sent between devices are 32-bit elements; how exact they have to be, the bound alone decides.
A program may use at most 192 MiB of HBM per device.

v0:
```python
import math

import jax
import jax.numpy as jnp
from jax import lax
from jax.sharding import PartitionSpec as P

WATER_SSA = 0.999
ICE_SSA = 0.99
WATER_ASYM = 0.85
ICE_ASYM = 0.78
DIFFUSIVITY = 1.66


def partner(block, axis, distance):
    count = lax.axis_size(axis)
    route = []
    for low in range(count):
        high = low | 1 << distance
        if high != low and high < count:
            route += [(low, high), (high, low)]
    return lax.ppermute(block, axis, route)


def surface_albedo(surface_kind, snow_cover, snow_age, surface_table, snow_table):
    kinds = jnp.arange(surface_table.shape[0], dtype=jnp.int32)
    onehot = (surface_kind[None, :] == kinds[:, None]).astype(jnp.float32)
    base_albedo = jnp.dot(surface_table.T, onehot, precision=lax.Precision.HIGHEST)
    snow_share = jnp.where(surface_kind >= 1, snow_cover, 0.0)
    fresh_snow = snow_table[:, None] * (1.0 - 0.5 * snow_age[None, :])
    return (1.0 - snow_share)[None, :] * base_albedo + snow_share[None, :] * fresh_snow


def optic_tables(gas_coeff, rayleigh, cloud_ext):
    gpt_count = gas_coeff.shape[1]
    cloud_gpt = jnp.repeat(cloud_ext, gpt_count // cloud_ext.shape[1], axis=1)
    gas_part = gas_coeff.T
    no_gas = jnp.zeros_like(gas_part)
    zero_col = jnp.zeros_like(rayleigh)
    extinct = jnp.concatenate([gas_part, jnp.stack([rayleigh, cloud_gpt[0], cloud_gpt[1]], 1)], 1)
    scatter = jnp.concatenate(
        [no_gas, jnp.stack([rayleigh, WATER_SSA * cloud_gpt[0], ICE_SSA * cloud_gpt[1]], 1)], 1
    )
    forward = jnp.concatenate(
        [
            no_gas,
            jnp.stack(
                [
                    zero_col,
                    WATER_ASYM * WATER_SSA * cloud_gpt[0],
                    ICE_ASYM * ICE_SSA * cloud_gpt[1],
                ],
                1,
            ),
        ],
        1,
    )
    return jnp.concatenate([extinct, scatter, forward], 0)


def radiate(amounts, albedo_band, cos_zen, optic_stack, solar_frac):
    levels, fields, width = amounts.shape
    gpt_count = solar_frac.shape[0]
    combined = jnp.einsum("kf,lfw->lkw", optic_stack, amounts, precision=lax.Precision.HIGHEST)
    depth = combined[:, :gpt_count]
    scatter = combined[:, gpt_count : 2 * gpt_count]
    forward = combined[:, 2 * gpt_count :]
    single = scatter / depth
    asymmetry = forward / scatter
    inv_cos = 1.0 / cos_zen
    diffuse_exp = jnp.exp(-DIFFUSIVITY * depth)
    beam_exp = jnp.exp(-depth * inv_cos[None, None, :])
    backward = 0.5 * single * (1.0 - asymmetry)
    onward = 0.5 * single * (1.0 + asymmetry)
    refl_diff = backward * (1.0 - diffuse_exp)
    tran_diff = diffuse_exp + onward * (1.0 - diffuse_exp)
    refl_dir = backward * (1.0 - beam_exp)
    scat_dir = onward * (1.0 - beam_exp)
    cum_depth = jnp.cumsum(depth, axis=0)
    depth_above = jnp.concatenate([jnp.zeros((1, gpt_count, width), jnp.float32), cum_depth], 0)
    direct = (
        solar_frac[None, :, None]
        * cos_zen[None, None, :]
        * jnp.exp(-depth_above * inv_cos[None, None, :])
    )
    ground_albedo = jnp.repeat(albedo_band, gpt_count // albedo_band.shape[0], axis=0)

    def upward(carried, inputs):
        alb_below, src_below = carried
        r_diff, t_diff, r_dir, s_dir, beam_top = inputs
        denom_inv = 1.0 / (1.0 - r_diff * alb_below)
        alb_here = r_diff + t_diff * t_diff * alb_below * denom_inv
        src_here = r_dir * beam_top + t_diff * denom_inv * (
            src_below + alb_below * s_dir * beam_top
        )
        return ((alb_here, src_here), (alb_below, src_below, denom_inv))

    (alb_top, src_top), (alb_next, src_next, denoms) = lax.scan(
        upward,
        (ground_albedo, ground_albedo * direct[-1]),
        (refl_diff, tran_diff, refl_dir, scat_dir, direct[:-1]),
        reverse=True,
    )
    net_top = direct[0] - src_top

    def downward(carried, inputs):
        down_flux, net_above = carried
        r_diff, t_diff, s_dir, beam_top, beam_bottom, alb_below, src_below, denom_inv = inputs
        down_below = (t_diff * down_flux + r_diff * src_below + s_dir * beam_top) * denom_inv
        up_below = alb_below * down_below + src_below
        net_below = down_below + beam_bottom - up_below
        return ((down_below, net_below), jnp.sum(net_above - net_below, axis=0))

    (down_ground, net_ground), absorbed = lax.scan(
        downward,
        (jnp.zeros_like(net_top), net_top),
        (refl_diff, tran_diff, scat_dir, direct[:-1], direct[1:], alb_next, src_next, denoms),
    )
    heat_rate = levels * absorbed / amounts[:, fields - 3, :]
    return (heat_rate, jnp.sum(net_ground, axis=0))


def build_columns(gases, masses, clouds, extras):
    amounts = jnp.concatenate(
        [jnp.swapaxes(gases, 0, 1), masses[:, None, :], jnp.swapaxes(clouds, 0, 1)], 1
    )
    levels, fields, width = amounts.shape
    return jnp.concatenate([amounts.reshape(levels * fields, width), extras], 0)


def compute_blocks(packed, levels, fields, optic_stack, solar_frac):
    width = packed.shape[1]
    block_width = math.gcd(width, 512)
    blocks = width // block_width
    amount_rows = levels * fields
    band_rows = packed.shape[0] - amount_rows - 2

    def one_block(block_index):
        col_block = lax.dynamic_slice_in_dim(packed, block_index * block_width, block_width, 1)
        amounts = col_block[:amount_rows].reshape(levels, fields, block_width)
        return radiate(
            amounts,
            col_block[amount_rows : amount_rows + band_rows],
            col_block[amount_rows + band_rows],
            optic_stack,
            solar_frac,
        )

    heat_blocks, flux_blocks = lax.map(one_block, jnp.arange(blocks, dtype=jnp.int32))
    return (jnp.swapaxes(heat_blocks, 0, 1).reshape(levels, width), flux_blocks.reshape(width))


def solve_columns(packed, levels, fields, optic_stack, solar_frac):
    width = packed.shape[1]
    half_cols = width // 2
    upper_side = lax.axis_index("pair") >= lax.axis_size("pair") // 2
    keep_start = jnp.where(upper_side, half_cols, 0)
    kept_cols = lax.dynamic_slice_in_dim(packed, keep_start, half_cols, 1)
    sent_cols = lax.dynamic_slice_in_dim(packed, half_cols - keep_start, half_cols, 1)
    pair_bit = lax.axis_size("pair").bit_length() - 2
    partner_cols = partner(sent_cols, "pair", pair_bit)
    own_lit = kept_cols[-1] > 0.5
    other_lit = partner_cols[-1] > 0.5
    merged = jnp.where(own_lit[None, :], kept_cols, partner_cols)
    heat_rate, surface_flux = compute_blocks(merged, levels, fields, optic_stack, solar_frac)
    results = jnp.concatenate([heat_rate, surface_flux[None, :]], 0)
    own_result = jnp.where(own_lit[None, :], results, 0.0)
    their_result = jnp.where(other_lit[None, :], results, 0.0)
    returned = partner(their_result, "pair", pair_bit)
    joined = jnp.where(
        upper_side,
        jnp.concatenate([returned, own_result], 1),
        jnp.concatenate([own_result, returned], 1),
    )
    return (joined[:-1], joined[-1])


def body(
    gas_amounts,
    layer_mass,
    cloud_paths,
    surface_kind,
    snow_cover,
    snow_age,
    cos_zenith,
    sunlit,
    gas_coeff,
    rayleigh,
    cloud_ext,
    surface_table,
    snow_table,
    solar_weight,
):
    levels = layer_mass.shape[0]
    fields = gas_amounts.shape[0] + 3
    optic_stack = optic_tables(gas_coeff, rayleigh, cloud_ext)
    solar_frac = solar_weight / jnp.sum(solar_weight)
    albedo_band = surface_albedo(surface_kind, snow_cover, snow_age, surface_table, snow_table)
    extras = jnp.concatenate(
        [albedo_band, cos_zenith[None, :], sunlit.astype(jnp.float32)[None, :]], 0
    )
    moved_gas, moved_mass = (
        lax.all_to_all(gas_amounts, "elem", split_axis=2, concat_axis=2, tiled=True),
        lax.all_to_all(layer_mass[None], "elem", split_axis=2, concat_axis=2, tiled=True),
    )
    packed = build_columns(moved_gas, moved_mass[0], cloud_paths, extras)
    heat_rate, surface_flux = solve_columns(packed, levels, fields, optic_stack, solar_frac)
    heating = lax.all_to_all(heat_rate, "elem", split_axis=1, concat_axis=1, tiled=True)
    return (heating, surface_flux)


def solution(mesh):
    placed = (
        P(None, None, ("pair", "elem")),
        P(None, ("pair", "elem")),
        P(None, None, ("pair", "elem")),
        P(("pair", "elem")),
        P(("pair", "elem")),
        P(("pair", "elem")),
        P(("pair", "elem")),
        P(("pair", "elem")),
        P(),
        P(),
        P(),
        P(),
        P(),
        P(),
    )
    return jax.shard_map(
        body,
        mesh=mesh,
        in_specs=placed,
        out_specs=(P(None, ("pair", "elem")), P(("pair", "elem"))),
        check_vma=False,
    )
```

profile of v0, /device:TPU:6, one launch (start us, length us, event | category | flops | bytes accessed | tf_op | source)
XLA Modules:
  0.0 566.6 jit_solution(11421891173453009880)
XLA Ops:
  2.6 9.3 %reduce.4 = f32[2048,24]{1,0:T(8,128)S(1)} reduce(f32[2048,1,24]{2,1,0:T(1,128)S(1)} %bitcast.194, f32[]{:T(128)} %broadcast.219), dimensions={1}, to_apply=%bitcast.129.reduce_sub_computation | reduce | bytes 393220
  13.4 11.5 %all-to-all-start.1 = ((f32[32,1,1536]{2,1,0:T(1,128)}), f32[32,1,1536]{2,1,0:T(1,128)S(1)}, u32[]{:S(2)}, u32[]{:S(2)}) async-start(f32[32,1,1536]{2,1,0:T(1,128)} %reshape.160), calls=%async_computation.1 | async-start | bytes 393216 | tf_op jit(solution)/shard_map/all_to_all | solution.py:204
  24.9 4.6 copy.40
  29.5 8.1 %reshape.162 = f32[32,1,10752]{2,1,0:T(1,128)} reshape(f32[2048,7,24]{2,1,0:T(8,128)} %bitcast.191) | data formatting | bytes 2752512
  37.7 10.1 %all-to-all-start = ((f32[32,1,10752]{2,1,0:T(1,128)}), f32[32,1,10752]{2,1,0:T(1,128)}, u32[]{:S(2)}, u32[]{:S(2)}) async-start(f32[32,1,10752]{2,1,0:T(1,128)} %reshape.162), calls=%async_computation | async-start | bytes 2752512 | tf_op jit(solution)/shard_map/all_to_all | solution.py:203
  49.8 2.0 reduce.5
  51.9 1.8 reshape.161
  54.8 27.3 %all-to-all-done = f32[32,1,10752]{2,1,0:T(1,128)} async-done(((f32[32,1,10752]{2,1,0:T(1,128)}), f32[32,1,10752]{2,1,0:T(1,128)}, u32[]{:S(2)}, u32[]{:S(2)}) %all-to-all-start) | async-done | bytes 1376288 | tf_op jit(solution)/shard_map/all_to_all | solution.py:203
  82.1 5.3 reduce.6
  87.5 5.9 %reshape.163 = f32[2048,7,24]{2,1,0:T(8,128)} reshape(f32[32,10752]{1,0:T(8,128)S(1)} %reduce.6) | data formatting | bytes 2752512
  93.4 3.8 bitcast_bitcast_fusion
  97.2 7.2 %pad_maximum_fusion = f32[24,10,2048]{0,1,2:T(8,128)} fusion(f32[24,2,2048]{0,1,2:T(2,128)S(1)} %bitcast.192, f32[24,1,2048]{0,1,2:T(1,128)S(1)} %copy-done.5, f32[24,7,2048]{0,1,2:T(8,128)S(1)} %bitcast_bitcast_fusion), kind=kLoop, calls=%fused_computation.53 | loop fusion | flops 983040 | bytes 3932160 | tf_op jit(solution)/shard_map/concatenate | solution.py:124
  104.4 10.5 %copy.43 = f32[24,10,2048]{2,1,0:T(8,128)S(1)} copy(f32[24,10,2048]{0,1,2:T(8,128)} %pad_maximum_fusion) | data formatting | bytes 3932160 | tf_op jit(solution)/shard_map/concatenate | solution.py:124
  121.6 20.1 %collective-permute-done = f32[256,1024]{1,0:T(8,128)} collective-permute-done((f32[256,1024]{1,0:T(8,128)S(1)}, f32[256,1024]{1,0:T(8,128)}, u32[]{:S(2)}, u32[]{:S(2)}) %collective-permute-start) | collective-permute-done | bytes 1048608 | tf_op jit(solution)/shard_map/ppermute | solution.py:22
  143.4 392.7 %while.109 = (s32[]{:T(128)}, f32[2,24,512]{2,1,0:T(8,128)S(1)}, f32[2,512]{1,0:T(2,128)S(1)}, f32[112]{0:T(128)S(1)}, s32[2]{0:T(128)S(1)}, /*index=5*/f32[256,...) while((s32[]{:T(128)}, f32[2,24,512]{2,1,0:T(8,128)S(1)}, ...), condition=%wide.region_9.10_spmd, body=%wide.region_1.9_spmd.sunk | while | flops 563658240 | bytes 243476912 | solution.py:149
  145.1 18.5 %convolution_bitcast_fusion.2 = f32[24,336,512]{2,1,0:T(8,128)S(1)} fusion(f32[24,10,512]{2,1,0:T(8,128)S(1)} %reshape.167, f32[336,10]{0,1:T(8,128)S(1)} %get-tuple-element.986), kind=kOutput, calls=%fused_computation.27.clone.1 | convolution fusion | flops 495452160 | bytes 17020032 | tf_op jit(solution)/shard_map/while/body/eval_jaxpr/kf,lfw->lkw/dot_general | solution.py:64
  163.6 5.6 copy-done.2
  169.3 2.7 fusion.42
  172.2 3.7 exponential_multiply_fusion.2
  175.9 11.2 %fusion.44 = (f32[24,112,512]{2,1,0:T(8,128)}, f32[24,112,512]{2,1,0:T(8,128)S(1)}, f32[24,112,512]{2,1,0:T(8,128)S(1)}) fusion(f32[24,336,512]{2,1,0:T(8,128)} %copy-done.2, f32[512]{0:T(512)S(1)} %broadcast_divide_fusion.3), kind=kLoop, calls=%fused_computation.37.clone.1 | loop fusion | flops 12386304 | bytes 33032192 | tf_op jit(solution)/shard_map/while/body/eval_jaxpr/mul | solution.py:78
  187.1 8.8 %fusion.45 = (f32[24,112,512]{2,1,0:T(8,128)}, f32[24,112,512]{2,1,0:T(8,128)}, f32[24,112,512]{2,1,0:T(8,128)}) fusion(f32[24,336,512]{2,1,0:T(8,128)} %copy-done.2, f32[512]{0:T(512)S(1)} %broadcast_divide_fusion.3, f32[24,112,512]{2,1,0:T(8,128)S(1)} %get-tuple-element.817, f32[24,112,512]{2,1,0:T(8,128)S(1)} %get-tuple-element.818), kind=kLoop, calls=%fused_computation.38.clone.1 | loop fusion | flops 17891328 | bytes 33032192 | tf_op jit(solution)/shard_map/while/body/eval_jaxpr/mul | solution.py:77
  196.0 6.0 %fusion.46 = (f32[24,112,512]{2,1,0:T(8,128)}, f32[24,112,512]{2,1,0:T(8,128)}) fusion(f32[25,112,512]{2,1,0:T(8,128)S(1)} %exponential_multiply_fusion.2), kind=kLoop, calls=%fused_computation.79.clone.1 | loop fusion | bytes 22020096 | tf_op jit(solution)/shard_map/while/body/eval_jaxpr/slice | solution.py:117
  202.0 3.1 broadcast.234
  205.0 3.1 broadcast.234.clone
  208.1 3.2 broadcast.234.clone.1
  211.3 81.8 %while.110 = (s32[]{:T(128)}, f32[112,512]{1,0:T(8,128)S(1)}, f32[112,512]{1,0:T(8,128)S(1)}, f32[24,112,512]{2,1,0:T(8,128)}, f32[24,112,512]{2,1,0:T(8,128)}, ...) while((s32[]{:T(128)}, f32[112,512]{1,0:T(8,128)S(1)}, ...), condition=%wide.region_4.4_spmd, body=%wide.region_3.3_spmd.sunk | while | flops 974851 | bytes 3440793 | solution.py:98
  211.3 1.9 bitcast_dynamic-update-slice_fusion.4
  214.7 1.9 bitcast_dynamic-update-slice_fusion.4
  221.5 1.8 bitcast_dynamic-update-slice_fusion.4
  225.0 1.9 bitcast_dynamic-update-slice_fusion.4
  231.8 1.8 bitcast_dynamic-update-slice_fusion.4
  245.4 1.9 bitcast_dynamic-update-slice_fusion.4
  248.9 1.8 bitcast_dynamic-update-slice_fusion.4
  252.3 1.8 bitcast_dynamic-update-slice_fusion.4
  262.5 1.8 bitcast_dynamic-update-slice_fusion.4
  272.6 1.9 bitcast_dynamic-update-slice_fusion.4
  282.8 1.8 bitcast_dynamic-update-slice_fusion.4
  294.0 45.6 %while.111 = (s32[]{:T(128)}, f32[112,512]{1,0:T(8,128)S(1)}, f32[112,512]{1,0:T(8,128)S(1)}, f32[24,512]{1,0:T(8,128)S(1)}, f32[24,112,512]{2,1,0:T(8,128)}, /*...) while((s32[]{:T(128)}, f32[112,512]{1,0:T(8,128)S(1)}, ...), condition=%wide.region_7.7_spmd.clone, body=%wide.region_5.6_spmd.clone.sunk | while | flops 744963 | bytes 2758815 | solution.py:114
  341.2 18.5 %convolution_bitcast_fusion.2 = f32[24,336,512]{2,1,0:T(8,128)S(1)} fusion(f32[24,10,512]{2,1,0:T(8,128)S(1)} %reshape.167, f32[336,10]{0,1:T(8,128)S(1)} %get-tuple-element.986), kind=kOutput, calls=%fused_computation.27.clone.1 | convolution fusion | flops 495452160 | bytes 17020032 | tf_op jit(solution)/shard_map/while/body/eval_jaxpr/kf,lfw->lkw/dot_general | solution.py:64
  359.7 5.6 copy-done.2
  365.4 2.7 fusion.42
  368.3 3.7 exponential_multiply_fusion.2
  372.0 11.2 %fusion.44 = (f32[24,112,512]{2,1,0:T(8,128)}, f32[24,112,512]{2,1,0:T(8,128)S(1)}, f32[24,112,512]{2,1,0:T(8,128)S(1)}) fusion(f32[24,336,512]{2,1,0:T(8,128)} %copy-done.2, f32[512]{0:T(512)S(1)} %broadcast_divide_fusion.3), kind=kLoop, calls=%fused_computation.37.clone.1 | loop fusion | flops 12386304 | bytes 33032192 | tf_op jit(solution)/shard_map/while/body/eval_jaxpr/mul | solution.py:78
  383.2 8.8 %fusion.45 = (f32[24,112,512]{2,1,0:T(8,128)}, f32[24,112,512]{2,1,0:T(8,128)}, f32[24,112,512]{2,1,0:T(8,128)}) fusion(f32[24,336,512]{2,1,0:T(8,128)} %copy-done.2, f32[512]{0:T(512)S(1)} %broadcast_divide_fusion.3, f32[24,112,512]{2,1,0:T(8,128)S(1)} %get-tuple-element.817, f32[24,112,512]{2,1,0:T(8,128)S(1)} %get-tuple-element.818), kind=kLoop, calls=%fused_computation.38.clone.1 | loop fusion | flops 17891328 | bytes 33032192 | tf_op jit(solution)/shard_map/while/body/eval_jaxpr/mul | solution.py:77
  392.1 6.0 %fusion.46 = (f32[24,112,512]{2,1,0:T(8,128)}, f32[24,112,512]{2,1,0:T(8,128)}) fusion(f32[25,112,512]{2,1,0:T(8,128)S(1)} %exponential_multiply_fusion.2), kind=kLoop, calls=%fused_computation.79.clone.1 | loop fusion | bytes 22020096 | tf_op jit(solution)/shard_map/while/body/eval_jaxpr/slice | solution.py:117
  398.1 3.1 broadcast.234
  401.1 3.1 broadcast.234.clone
  404.2 3.2 broadcast.234.clone.1
  407.4 81.8 %while.110 = (s32[]{:T(128)}, f32[112,512]{1,0:T(8,128)S(1)}, f32[112,512]{1,0:T(8,128)S(1)}, f32[24,112,512]{2,1,0:T(8,128)}, f32[24,112,512]{2,1,0:T(8,128)}, ...) while((s32[]{:T(128)}, f32[112,512]{1,0:T(8,128)S(1)}, ...), condition=%wide.region_4.4_spmd, body=%wide.region_3.3_spmd.sunk | while | flops 974851 | bytes 3440793 | solution.py:98
  407.4 1.9 bitcast_dynamic-update-slice_fusion.4
  410.8 1.9 bitcast_dynamic-update-slice_fusion.4
  417.7 1.8 bitcast_dynamic-update-slice_fusion.4
  421.1 1.9 bitcast_dynamic-update-slice_fusion.4
  427.9 1.8 bitcast_dynamic-update-slice_fusion.4
  441.5 1.9 bitcast_dynamic-update-slice_fusion.4
  445.0 1.8 bitcast_dynamic-update-slice_fusion.4
  448.4 1.8 bitcast_dynamic-update-slice_fusion.4
  458.6 1.8 bitcast_dynamic-update-slice_fusion.4
  468.7 1.9 bitcast_dynamic-update-slice_fusion.4
  479.0 1.8 bitcast_dynamic-update-slice_fusion.4
  490.1 45.6 %while.111 = (s32[]{:T(128)}, f32[112,512]{1,0:T(8,128)S(1)}, f32[112,512]{1,0:T(8,128)S(1)}, f32[24,512]{1,0:T(8,128)S(1)}, f32[24,112,512]{2,1,0:T(8,128)}, /*...) while((s32[]{:T(128)}, f32[112,512]{1,0:T(8,128)S(1)}, ...), condition=%wide.region_7.7_spmd.clone, body=%wide.region_5.6_spmd.clone.sunk | while | flops 744963 | bytes 2758815 | solution.py:114
  539.3 5.1 collective-permute-done.1
  545.7 7.5 %all-to-all-start.2 = ((f32[32,1,1536]{2,1,0:T(1,128)}), f32[32,1,1536]{2,1,0:T(1,128)S(1)}, u32[]{:S(2)}, u32[]{:S(2)}) async-start(f32[32,1,1536]{2,1,0:T(1,128)} %reshape.164), calls=%async_computation.2 | async-start | bytes 393216 | tf_op jit(solution)/shard_map/all_to_all | solution.py:208
  553.8 10.3 %all-to-all-done.2 = f32[32,1,1536]{2,1,0:T(1,128)S(1)} async-done(((f32[32,1,1536]{2,1,0:T(1,128)}), f32[32,1,1536]{2,1,0:T(1,128)S(1)}, u32[]{:S(2)}, u32[]{:S(2)}) %all-to-all-start.2) | async-done | bytes 196640 | tf_op jit(solution)/shard_map/all_to_all | solution.py:208
  (292 shorter events, 237.9 us)
Async XLA Ops:
  0.6 48.3 %copy-start = (f32[4,14]{1,0:T(4,128)S(1)}, f32[4,14]{1,0:T(4,128)}, u32[]{:S(2)}) copy-start(f32[4,14]{1,0:T(4,128)} %param.31) | copy-start | bytes 676
  0.6 24.2 %copy-start.6 = (f32[7,24,2048]{2,1,0:T(8,128)S(1)}, f32[7,24,2048]{2,1,0:T(8,128)}, u32[]{:S(2)}) copy-start(f32[7,24,2048]{2,1,0:T(8,128)} %param.20) | copy-start | bytes 4128772
  13.4 24.3 %all-to-all-start.1 = ((f32[32,1,1536]{2,1,0:T(1,128)}), f32[32,1,1536]{2,1,0:T(1,128)S(1)}, u32[]{:S(2)}, u32[]{:S(2)}) async-start(f32[32,1,1536]{2,1,0:T(1,128)} %reshape.160), calls=%async_computation.1 | async-start | bytes 393216 | tf_op jit(solution)/shard_map/all_to_all | solution.py:204
  29.5 18.2 %copy-start.12 = (s32[2048]{0:T(1024)S(1)}, s32[2048]{0:T(1024)}, u32[]{:S(2)}) copy-start(s32[2048]{0:T(1024)} %param.27) | copy-start | bytes 24580
  29.5 18.3 %copy-start.8 = (f32[2,24,2048]{2,1,0:T(8,128)S(1)}, f32[2,24,2048]{2,1,0:T(8,128)}, u32[]{:S(2)}) copy-start(f32[2,24,2048]{2,1,0:T(8,128)} %param.22) | copy-start | bytes 1179652
  29.5 19.3 %copy-start.13 = (f32[2048]{0:T(1024)S(1)}, f32[2048]{0:T(1024)}, u32[]{:S(2)}) copy-start(f32[2048]{0:T(1024)} %param.24) | copy-start | bytes 24580
  29.5 19.3 %copy-start.14 = (f32[2048]{0:T(1024)S(1)}, f32[2048]{0:T(1024)}, u32[]{:S(2)}) copy-start(f32[2048]{0:T(1024)} %param.25) | copy-start | bytes 24580
  29.5 19.3 %copy-start.15 = (s32[2048]{0:T(1024)S(1)}, s32[2048]{0:T(1024)}, u32[]{:S(2)}) copy-start(s32[2048]{0:T(1024)} %param.23) | copy-start | bytes 24580
  29.5 19.4 %copy-start.19 = (f32[14]{0:T(128)S(1)}, f32[14]{0:T(128)}, u32[]{:S(2)}) copy-start(f32[14]{0:T(128)} %param.32) | copy-start | bytes 172
  37.7 10.1 %copy-start.7 = (f32[32,1,1536]{2,1,0:T(1,128)}, f32[32,1,1536]{2,1,0:T(1,128)S(1)}, u32[]{:S(2)}) copy-start(f32[32,1,1536]{2,1,0:T(1,128)S(1)} %all-to-all-done.1) | copy-start | bytes 589828
  37.7 44.5 %all-to-all-start = ((f32[32,1,10752]{2,1,0:T(1,128)}), f32[32,1,10752]{2,1,0:T(1,128)}, u32[]{:S(2)}, u32[]{:S(2)}) async-start(f32[32,1,10752]{2,1,0:T(1,128)} %reshape.162), calls=%async_computation | async-start | bytes 2752512 | tf_op jit(solution)/shard_map/all_to_all | solution.py:203
  93.4 3.8 copy-start.5
  104.4 12.0 %copy-start.9 = (f32[14,2048]{1,0:T(8,128)S(1)}, f32[14,2048]{1,0:T(8,128)}, u32[]{:S(2)}) copy-start(f32[14,2048]{1,0:T(8,128)} %fusion.22) | copy-start | bytes 344068
  104.4 12.1 %copy-start.11 = (f32[2048]{0:T(1024)S(1)}, f32[2048]{0:T(1024)}, u32[]{:S(2)}) copy-start(f32[2048]{0:T(1024)} %param.26) | copy-start | bytes 24580
  114.9 4.9 copy-start.17
  115.0 5.2 copy-start.20
  115.0 5.8 %copy-start.16 = (f32[7,112]{1,0:T(8,128)S(1)}, f32[7,112]{1,0:T(8,128)}, u32[]{:S(2)}) copy-start(f32[7,112]{1,0:T(8,128)} %param.28) | copy-start | bytes 9412
  115.0 5.8 %copy-start.18 = (f32[112]{0:T(128)S(1)}, f32[112]{0:T(128)}, u32[]{:S(2)}) copy-start(f32[112]{0:T(128)} %param.29) | copy-start | bytes 1348
  118.2 3.5 copy-start.4
  118.3 23.4 %collective-permute-start = (f32[256,1024]{1,0:T(8,128)S(1)}, f32[256,1024]{1,0:T(8,128)}, u32[]{:S(2)}, u32[]{:S(2)}) collective-permute-start(f32[256,1024]{1,0:T(8,128)S(1)} %constant_dynamic-slice_fusion.1), channel_id=1, source_target_pairs={{0,128},{128,0},{32,160},{160,32},{64,192},{192,64},{96,224},{224,... | collective-permute-start | bytes 3145736 | tf_op jit(solution)/shard_map/ppermute | solution.py:22
  121.6 21.8 %copy-start.10 = (pred[1024]{0:T(1024)(128)(4,1)}, pred[1024]{0:T(1024)(128)(4,1)S(1)}, u32[]{:S(2)}) copy-start(pred[1024]{0:T(1024)(128)(4,1)S(1)} %compare_reduce_fusion) | copy-start | bytes 3076
  163.6 5.7 copy-start.2
  175.8 20.1 %copy-start.3 = (f32[25,112,512]{2,1,0:T(8,128)}, f32[25,112,512]{2,1,0:T(8,128)S(1)}, u32[]{:S(2)}) copy-start(f32[25,112,512]{2,1,0:T(8,128)S(1)} %exponential_multiply_fusion.2) | copy-start | bytes 17203204 | tf_op jit(solution)/shard_map/while
  359.7 5.7 copy-start.2
  372.0 20.1 %copy-start.3 = (f32[25,112,512]{2,1,0:T(8,128)}, f32[25,112,512]{2,1,0:T(8,128)S(1)}, u32[]{:S(2)}) copy-start(f32[25,112,512]{2,1,0:T(8,128)S(1)} %exponential_multiply_fusion.2) | copy-start | bytes 17203204 | tf_op jit(solution)/shard_map/while
  536.1 30.1 %copy-start.1 = (f32[4,14]{1,0:T(4,128)S(1)}, f32[4,14]{1,0:T(4,128)}, u32[]{:S(2)}) copy-start(f32[4,14]{1,0:T(4,128)} %param.31) | copy-start | bytes 676
  537.8 6.6 %collective-permute-start.1 = (f32[25,1024]{1,0:T(8,128)S(1)}, f32[25,1024]{1,0:T(8,128)S(1)}, u32[]{:S(2)}, u32[]{:S(2)}) collective-permute-start(f32[25,1024]{1,0:T(8,128)S(1)} %get-tuple-element.578), channel_id=1, source_target_pairs={{0,128},{128,0},{32,160},{160,32},{64,192},{192,64},{96,224},{224,... | collective-permute-start | bytes 307208 | tf_op jit(solution)/shard_map/ppermute | solution.py:22
  545.7 18.4 %all-to-all-start.2 = ((f32[32,1,1536]{2,1,0:T(1,128)}), f32[32,1,1536]{2,1,0:T(1,128)S(1)}, u32[]{:S(2)}, u32[]{:S(2)}) async-start(f32[32,1,1536]{2,1,0:T(1,128)} %reshape.164), calls=%async_computation.2 | async-start | bytes 393216 | tf_op jit(solution)/shard_map/all_to_all | solution.py:208
where the time goes:
time: 578 us; the launch traced here: 567 us
  other arithmetic  336 us (58%)
  local copies, waits for them, and re-layouts  91.9 us (16%)
  waiting for transfers between devices  62.8 us (11%)
  matrix products  37.9 us (7%)
  starting transfers between devices  32 us (6%)
    dynamic_update_slice x48, other arithmetic, radiate(): lax.scan(upward, (ground_albedo, ground_albedo * direct[-1]), (refl_diff,...  87.9 us
    reduce_sum x48, other arithmetic, downward(): return ((down_below, net_below), jnp.sum(net_above - net_below, axis=0))  87.2 us
    add x48, other arithmetic, upward(): r_dir * beam_top  74.7 us
    dot_general x2, matrix products, radiate(): jnp.einsum('kf,lfw->lkw', optic_stack, amounts, precision=lax.Precision.H...  36.9 us
    all_to_all x1, waiting for transfers between devices, body(): lax.all_to_all(gas_amounts, 'elem', split_axis=2, concat_axis=2, tiled=True)  27.3 us
    unnamed x50, local copies, waits for them, and re-layouts  26.1 us
    ppermute x2, waiting for transfers between devices, partner(): return lax.ppermute(block, axis, route)  25.1 us
    mul x2, other arithmetic, radiate(): scat_dir = onward * (1.0 - beam_exp)  22.5 us
  transfers between devices with their start and end apart: 5, of which 4 were waited for; matrix products, arithmetic and copies ran while one was open for 4% of the time, Pallas kernels for 0%

commit v1 on v0

v1 whole, which is shorter than its diff:
```python
import functools

import jax
import jax.numpy as jnp
from jax import lax
from jax.experimental import pallas as pl
from jax.experimental.pallas import tpu as pltpu
from jax.sharding import PartitionSpec as P

WATER_SSA = 0.999
ICE_SSA = 0.99
WATER_ASYM = 0.85
ICE_ASYM = 0.78
DIFFUSIVITY = 1.66
LOG2E = 1.4426950408889634

F32 = jnp.float32
BF16 = jnp.bfloat16
LANES = 128
HALF = 64
GPTS = 112
BANDS = 14
LEVELS = 24
GASES = 7
FIELD_ROWS = 8 * LEVELS
PACKED_ROWS = FIELD_ROWS // 2
STATE_ROWS = 56
STEPS = 8
UNROLL = 24
MESH = pl.DeviceIdType.MESH


def split3(x):
    first = x.astype(BF16).astype(F32)
    rest = x - first
    second = rest.astype(BF16).astype(F32)
    return first, second, rest - second


def lane_pad(x):
    return jnp.concatenate([x, jnp.zeros((x.shape[0], LANES - x.shape[1]), F32)], 1)


def make_tables(gas, ray, cloud, solar, surface, snow, coef_ref, solar_ref, albtab_ref):
    shape = (BANDS, LANES)
    band = lax.broadcasted_iota(jnp.int32, shape, 1) // 8 == lax.broadcasted_iota(jnp.int32, shape, 0)
    cloud_gpt = jnp.dot(
        cloud, band.astype(F32), precision=lax.Precision.HIGHEST, preferred_element_type=F32
    )
    ray = lane_pad(ray)
    water, ice = WATER_SSA * cloud_gpt[0:1], ICE_SSA * cloud_gpt[1:2]
    zero6, zero7, zero32 = (jnp.zeros((n, LANES), F32) for n in (6, 7, 32))
    stacks = (
        [lane_pad(gas), ray, cloud_gpt, zero6],
        [zero7, 0.5 * ray, 0.5 * (1 - WATER_ASYM) * water, 0.5 * (1 - ICE_ASYM) * ice, zero6],
        [zero7, 0.5 * ray, 0.5 * (1 + WATER_ASYM) * water, 0.5 * (1 + ICE_ASYM) * ice, zero6],
    )
    for index, stack in enumerate(stacks):
        a1, a2, a3 = split3(jnp.concatenate(stack, 0))
        terms = jnp.concatenate([a1, a1, a2, a1, a3, a2, zero32], 0)
        coef_ref[pl.ds(index * GPTS, GPTS), :] = jnp.transpose(terms)[:GPTS].astype(BF16)
    solar = lane_pad(solar)
    solar = solar / jnp.sum(solar)
    square = (LANES, LANES)
    solar_ref[...] = jnp.transpose(jnp.broadcast_to(solar, square))[:GPTS]
    rows = jnp.concatenate([lane_pad(surface), lane_pad(snow)], 0)
    for index in range(5):
        albtab_ref[pl.ds(index * 16, 16), :] = jnp.transpose(
            jnp.broadcast_to(rows[index : index + 1], square)
        )[:16]


def compute_tile(x_ref, state, coef_ref, solar_ref, albtab_ref, alb_ref, layer_ref, net_ref):
    block = (8, LANES)
    kind, share, age, cosine = state[0:1], state[1:2], state[2:3], state[3:4]
    beam_scale = jnp.broadcast_to(-LOG2E / cosine, block)
    base = jnp.zeros((16, LANES), F32)
    for index in range(4):
        base = jnp.where(kind == float(index), albtab_ref[pl.ds(index * 16, 16), :], base)
    fresh = albtab_ref[pl.ds(64, 16), :] * (1.0 - 0.5 * age)
    alb_ref[...] = (1.0 - share) * base + share * fresh

    def upward(step, carried):
        alb, src = carried
        layer = LEVELS - 1 - step
        x1, x2, x3 = split3(x_ref[pl.ds(layer, 16, stride=LEVELS), :])
        terms = jnp.concatenate([x1, x2, x1, x3, x1, x2, jnp.zeros((32, LANES), F32)], 0)
        optics = jnp.dot(coef_ref[...], terms.astype(BF16), preferred_element_type=F32)
        next_alb, next_src = [], []
        for b in range(BANDS):
            depth = optics[8 * b : 8 * b + 8]
            inv_depth = pl.reciprocal(depth, approx=True)
            backward = optics[GPTS + 8 * b : GPTS + 8 * b + 8] * inv_depth
            onward = optics[2 * GPTS + 8 * b : 2 * GPTS + 8 * b + 8] * inv_depth
            diffuse_exp = jnp.exp2(depth * (-DIFFUSIVITY * LOG2E))
            beam_exp = jnp.exp2(depth * beam_scale)
            diffuse_loss = 1.0 - diffuse_exp
            beam_loss = 1.0 - beam_exp
            refl_diff = backward * diffuse_loss
            tran_diff = diffuse_exp + onward * diffuse_loss
            refl_dir = backward * beam_loss
            scat_dir = onward * beam_loss
            denom = pl.reciprocal(1.0 - refl_diff * alb[b], approx=True)
            through = tran_diff * denom
            src_beam = src[b] * beam_exp
            gain = (refl_diff * src_beam + scat_dir) * denom
            src_here = refl_dir + through * (src_beam + alb[b] * scat_dir)
            alb_here = refl_diff + tran_diff * through * alb[b]
            layer_ref[layer, 0, b] = through
            layer_ref[layer, 1, b] = gain
            layer_ref[layer, 2, b] = beam_exp
            layer_ref[layer, 3, b] = 1.0 - alb_here
            layer_ref[layer, 4, b] = 1.0 - src_here
            next_alb.append(alb_here)
            next_src.append(src_here)
        return tuple(next_alb), tuple(next_src)

    ground = tuple(jnp.broadcast_to(alb_ref[b : b + 1, :], block) for b in range(BANDS))
    lax.fori_loop(0, LEVELS, upward, (ground, ground), unroll=UNROLL)

    def downward(layer, carried):
        down, direct = carried
        net = jnp.zeros(block, F32)
        next_down, next_direct = [], []
        for b in range(BANDS):
            net = net + (layer_ref[layer, 3, b] * down[b] + layer_ref[layer, 4, b] * direct[b])
            next_down.append(layer_ref[layer, 0, b] * down[b] + layer_ref[layer, 1, b] * direct[b])
            next_direct.append(layer_ref[layer, 2, b] * direct[b])
        net_ref[layer] = net
        return tuple(next_down), tuple(next_direct)

    beam = tuple(solar_ref[pl.ds(8 * b, 8), :] * cosine for b in range(BANDS))
    none = tuple(jnp.zeros(block, F32) for b in range(BANDS))
    down, direct = lax.fori_loop(0, LEVELS, downward, (none, beam), unroll=UNROLL)
    net = jnp.zeros(block, F32)
    for b in range(BANDS):
        net = net + (1.0 - jnp.broadcast_to(alb_ref[b : b + 1, :], block)) * (down[b] + direct[b])
    net_ref[LEVELS] = net
    nets = jnp.sum(net_ref[...], axis=1)
    mass = x_ref[pl.ds(GASES * LEVELS, LEVELS), :]
    return float(LEVELS) * (nets[:LEVELS] - nets[1:]) / mass, nets[LEVELS:]


def kernel(
    gas_ref, mass_ref, cloud_ref, kind_ref, cover_ref, age_ref, cosine_ref, lit_ref,
    coeff_ref, ray_ref, cext_ref, surface_ref, snow_ref, weight_ref,
    heat_ref, flux_ref,
    send, recv, state, their_state, result, returned, flux_out, flux_in,
    x_ref, coef_ref, solar_ref, albtab_ref, alb_ref, layer_ref, net_ref,
    send_sem, recv_sem, state_send, state_recv, result_send, result_recv, fluxo_sem, fluxi_sem,
):
    pair, elem = lax.axis_index("pair"), lax.axis_index("elem")
    half_pairs = lax.axis_size("pair") // 2
    side, group = pair // half_pairs, pair % half_pairs
    z, y = elem // 4, elem % 4
    y_pair, y_low = y // 2, y % 2
    other = 1 - side
    partner = (other * half_pairs + group, elem)

    def device(which_side, which_elem):
        return (which_side * half_pairs + group, which_elem)

    barrier = pltpu.get_barrier_semaphore()

    def greet_other(k, _):
        pl.semaphore_signal(barrier, inc=1, device_id=device(other, k), device_id_type=MESH)
        return 0

    def greet_own(index, _):
        k = ((z + 2 * (index // 4) + side) % 8) * 4 + index % 4

        @pl.when(k != elem)
        def _():
            pl.semaphore_signal(barrier, inc=1, device_id=device(side, k), device_id_type=MESH)

        return 0

    lax.fori_loop(0, 32, greet_other, 0)
    lax.fori_loop(0, 16, greet_own, 0)

    for tile in range(16):
        state[tile, 0:48, :] = cloud_ref[:, tile * LANES : (tile + 1) * LANES]
        kind = kind_ref[tile : tile + 1, :]
        state[tile, 48:49, :] = kind.astype(F32)
        state[tile, 49:50, :] = jnp.where(kind >= 1, cover_ref[tile : tile + 1, :], 0.0)
        state[tile, 50:51, :] = age_ref[tile : tile + 1, :]
        state[tile, 51:52, :] = cosine_ref[tile : tile + 1, :]
        state[tile, 52:53, :] = lit_ref[tile : tile + 1, :].astype(F32)
        state[tile, 53:56, :] = jnp.zeros((3, LANES), F32)
    x_ref[...] = jnp.zeros_like(x_ref)

    pl.semaphore_wait(barrier, 47 + side)

    low_half = lax.broadcasted_iota(jnp.int32, (PACKED_ROWS, LANES), 1) < HALF
    low_half8 = lax.broadcasted_iota(jnp.int32, (8, LANES), 1) < HALF
    low_half24 = lax.broadcasted_iota(jnp.int32, (LEVELS, LANES), 1) < HALF

    def tile_of(step, which_side, sign):
        z_step = 2 * (step // 2) + which_side
        return ((z + 8 + sign * z_step) % 8) * 2 + (y_pair + step % 2) % 2

    def gas_copy(step, which_side, k):
        return pltpu.make_async_remote_copy(
            src_ref=send.at[k],
            dst_ref=recv.at[side, step, y_low],
            send_sem=send_sem.at[k],
            recv_sem=recv_sem.at[side, step, y_low],
            device_id=device(which_side, k),
            device_id_type=MESH,
        )

    def send_gas(index, _):
        step, which_side = index // 2, index % 2
        tile = tile_of(step, which_side, 1)
        columns = pl.ds(pl.multiple_of(tile * LANES, LANES), LANES)
        first = gas_ref[0:PACKED_ROWS, columns]
        second = jnp.concatenate([gas_ref[PACKED_ROWS : GASES * LEVELS, columns], mass_ref[:, columns]], 0)
        send[2 * tile] = jnp.where(low_half, first, pltpu.roll(second, HALF, 1))
        send[2 * tile + 1] = jnp.where(low_half, pltpu.roll(first, HALF, 1), second)
        for low in range(2):
            k = 2 * tile + low
            local = jnp.logical_and(which_side == side, k == elem)

            @pl.when(jnp.logical_not(local))
            def _():
                gas_copy(step, which_side, k).start()

            @pl.when(local)
            def _():
                pltpu.make_async_copy(
                    send.at[k], recv.at[side, step, y_low], recv_sem.at[side, step, y_low]
                ).start()

        return 0

    def state_copy(step):
        return pltpu.make_async_remote_copy(
            src_ref=state.at[tile_of(step, other, -1)],
            dst_ref=their_state.at[step],
            send_sem=state_send.at[step],
            recv_sem=state_recv.at[step],
            device_id=partner,
            device_id_type=MESH,
        )

    def send_state(step, _):
        state_copy(step).start()
        return 0

    lax.fori_loop(0, 4, send_gas, 0)
    lax.fori_loop(0, STEPS, send_state, 0)
    lax.fori_loop(4, 16, send_gas, 0)

    make_tables(
        coeff_ref[...], ray_ref[...], cext_ref[...], weight_ref[...], surface_ref[...], snow_ref[...],
        coef_ref, solar_ref, albtab_ref,
    )

    def result_copy(step, which_side, low):
        element = 2 * tile_of(step, side, -1) + low
        return element, pltpu.make_async_remote_copy(
            src_ref=result.at[step, which_side, (low + y_low) % 2],
            dst_ref=returned.at[elem],
            send_sem=result_send.at[step, which_side, low],
            recv_sem=result_recv.at[elem],
            device_id=device(which_side, element),
            device_id_type=MESH,
        )

    def flux_copy(step):
        return pltpu.make_async_remote_copy(
            src_ref=flux_out.at[step],
            dst_ref=flux_in.at[step],
            send_sem=fluxo_sem.at[step],
            recv_sem=fluxi_sem.at[step],
            device_id=partner,
            device_id_type=MESH,
        )

    def both_halves(row):
        row = jnp.broadcast_to(row, (8, LANES))
        turned = pltpu.roll(row, HALF, 1)
        return jnp.where(low_half8, row, turned)[0:1], jnp.where(low_half8, turned, row)[0:1]

    def one_tile(step, _):
        tile = tile_of(step, side, -1)
        state_copy(step).wait_recv()
        for which_side in range(2):
            for low in range(2):
                pltpu.make_async_copy(
                    recv.at[which_side, step, low],
                    recv.at[which_side, step, low],
                    recv_sem.at[which_side, step, low],
                ).wait()
        mine, theirs = state[tile], their_state[step]
        own_lit, other_lit = mine[52:53], theirs[52:53]
        merged = jnp.where(own_lit > 0.5, mine, theirs)
        mask0, mask1 = both_halves(own_lit)
        part0 = jnp.where(mask0 > 0.5, recv[side, step, 0], recv[other, step, 0])
        part1 = jnp.where(mask1 > 0.5, recv[side, step, 1], recv[other, step, 1])
        x_ref[pl.ds(0, PACKED_ROWS), :] = jnp.where(low_half, part0, pltpu.roll(part1, HALF, 1))
        x_ref[pl.ds(PACKED_ROWS, PACKED_ROWS), :] = jnp.where(low_half, pltpu.roll(part0, HALF, 1), part1)
        x_ref[pl.ds(FIELD_ROWS, 2 * LEVELS), :] = merged[0 : 2 * LEVELS]
        heat, flux = compute_tile(
            x_ref, merged[2 * LEVELS :], coef_ref, solar_ref, albtab_ref, alb_ref, layer_ref, net_ref
        )
        flux_ref[pl.ds(tile, 1), :] = jnp.where(own_lit > 0.5, flux, 0.0)
        flux_out[step] = jnp.broadcast_to(jnp.where(other_lit > 0.5, flux, 0.0), (8, LANES))
        flux_copy(step).start()
        for which_side in range(2):
            lit = jnp.where(which_side == side, own_lit, other_lit) > 0.5
            kept = jnp.where(lit, heat, 0.0)
            result[step, which_side, 0] = kept
            result[step, which_side, 1] = pltpu.roll(kept, HALF, 1)
            for low in range(2):
                element, copy = result_copy(step, which_side, low)
                local = jnp.logical_and(which_side == side, element == elem)

                @pl.when(jnp.logical_not(local))
                def _():
                    copy.start()

                @pl.when(local)
                def _():
                    pltpu.make_async_copy(
                        result.at[step, which_side, (low + y_low) % 2],
                        returned.at[elem],
                        result_recv.at[elem],
                    ).start()

        return 0

    lax.fori_loop(0, STEPS, one_tile, 0)

    def finish_flux(step, _):
        flux_copy(step).wait()
        flux_ref[pl.ds(tile_of(step, other, -1), 1), :] = flux_in[step, 0:1, :]
        state_copy(step).wait_send()
        for which_side in range(2):
            for low in range(2):
                element, copy = result_copy(step, which_side, low)
                local = jnp.logical_and(which_side == side, element == elem)

                @pl.when(jnp.logical_not(local))
                def _():
                    copy.wait_send()

        return 0

    def finish_gas(index, _):
        step, which_side = index // 2, index % 2
        tile = tile_of(step, which_side, 1)
        for low in range(2):
            k = 2 * tile + low
            local = jnp.logical_and(which_side == side, k == elem)

            @pl.when(jnp.logical_not(local))
            def _():
                gas_copy(step, which_side, k).wait_send()

        return 0

    def finish_heat(tile, _):
        for low in range(2):
            pltpu.make_async_copy(
                returned.at[2 * tile + low], returned.at[2 * tile + low], result_recv.at[2 * tile + low]
            ).wait()
        columns = pl.ds(pl.multiple_of(tile * LANES, LANES), LANES)
        heat_ref[:, columns] = jnp.where(low_half24, returned[2 * tile], returned[2 * tile + 1])
        return 0

    lax.fori_loop(0, 16, finish_gas, 0)
    lax.fori_loop(0, STEPS, finish_flux, 0)
    lax.fori_loop(0, 16, finish_heat, 0)


def body(
    gas_amounts, layer_mass, cloud_paths, surface_kind, snow_cover, snow_age, cos_zenith, sunlit,
    gas_coeff, rayleigh, cloud_ext, surface_table, snow_table, solar_weight,
):
    width = layer_mass.shape[1]
    rows = lambda x: x.reshape(width // LANES, LANES)
    vmem = pl.BlockSpec(memory_space=pltpu.VMEM)
    dma = pltpu.SemaphoreType.DMA
    heating, flux = pl.pallas_call(
        kernel,
        out_shape=(
            jax.ShapeDtypeStruct((LEVELS, width), F32),
            jax.ShapeDtypeStruct((width // LANES, LANES), F32),
        ),
        in_specs=[vmem] * 14,
        out_specs=(vmem, vmem),
        scratch_shapes=[
            pltpu.VMEM((32, PACKED_ROWS, LANES), F32),
            pltpu.VMEM((2, STEPS, 2, PACKED_ROWS, LANES), F32),
            pltpu.VMEM((16, STATE_ROWS, LANES), F32),
            pltpu.VMEM((STEPS, STATE_ROWS, LANES), F32),
            pltpu.VMEM((STEPS, 2, 2, LEVELS, LANES), F32),
            pltpu.VMEM((32, LEVELS, LANES), F32),
            pltpu.VMEM((STEPS, 8, LANES), F32),
            pltpu.VMEM((STEPS, 8, LANES), F32),
            pltpu.VMEM((16 * LEVELS, LANES), F32),
            pltpu.VMEM((3 * GPTS, LANES), BF16),
            pltpu.VMEM((GPTS, LANES), F32),
            pltpu.VMEM((80, LANES), F32),
            pltpu.VMEM((16, LANES), F32),
            pltpu.VMEM((LEVELS, 5, BANDS, 8, LANES), F32),
            pltpu.VMEM((LEVELS + 1, 8, LANES), F32),
            dma((32,)),
            dma((2, STEPS, 2)),
            dma((STEPS,)),
            dma((STEPS,)),
            dma((STEPS, 2, 2)),
            dma((32,)),
            dma((STEPS,)),
            dma((STEPS,)),
        ],
        compiler_params=pltpu.CompilerParams(
            collective_id=0, has_side_effects=True, vmem_limit_bytes=40 * 2**20
        ),
    )(
        gas_amounts.reshape(GASES * LEVELS, width),
        layer_mass,
        cloud_paths.reshape(2 * LEVELS, width),
        rows(surface_kind), rows(snow_cover), rows(snow_age), rows(cos_zenith), rows(sunlit),
        gas_coeff, rayleigh.reshape(1, GPTS), cloud_ext, surface_table,
        snow_table.reshape(1, BANDS), solar_weight.reshape(1, GPTS),
    )
    return heating, flux.reshape(width)


def solution(mesh):
    columns = ("pair", "elem")
    placed = (
        P(None, None, columns), P(None, columns), P(None, None, columns),
        P(columns), P(columns), P(columns), P(columns), P(columns),
        P(), P(), P(), P(), P(), P(),
    )
    return jax.shard_map(
        body,
        mesh=mesh,
        in_specs=placed,
        out_specs=(P(None, columns), P(columns)),
        check_vma=False,
    )
```

time: 578 us -> 83.3 us (0.14); the launches traced: 567 us -> 82.8 us
  other arithmetic: 336 us -> 0 us
  local copies, waits for them, and re-layouts: 91.9 us -> 12 us
  Pallas kernels: 0 us -> 70.1 us
  waiting for transfers between devices: 62.8 us -> 0 us
  matrix products: 37.9 us -> 0 us
  starting transfers between devices: 32 us -> 0 us
    dynamic_update_slice x50 -> x0, other arithmetic: 88 us -> none  [the longest x48 87.9 us: radiate(): lax.scan(upward, (ground_albedo, ground_albedo * direct[-1]), (refl_diff,...]
    reduce_sum x51 -> x0, other arithmetic: 87.9 us -> none  [the longest x48 87.2 us: downward(): return ((down_below, net_below), jnp.sum(net_above - net_below, axis=0))]
    add x48 -> x0, other arithmetic: 74.7 us -> none  [upward(): r_dir * beam_top]
    pallas_call x0 -> x1, Pallas kernels: none -> 70.1 us  [body(): pl.pallas_call(kernel, out_shape=(jax.ShapeDtypeStruct((LEVELS, width), F...]
    mul x11 -> x0, other arithmetic: 47.7 us -> none  [the longest x2 22.5 us: radiate(): scat_dir = onward * (1.0 - beam_exp)]
    dot_general x3 -> x0, matrix products: 37.9 us -> none  [the longest x2 36.9 us: radiate(): jnp.einsum('kf,lfw->lkw', optic_stack, amounts, precision=lax.Precision.H...]
    all_to_all x3 -> x0, waiting for transfers between devices: 37.6 us -> none  [the longest x1 27.3 us: body(): lax.all_to_all(gas_amounts, 'elem', split_axis=2, concat_axis=2, tiled=True)]
    all_to_all x3 -> x0, starting transfers between devices: 29 us -> none  [the longest x1 11.5 us: body(): lax.all_to_all(layer_mass[None], 'elem', split_axis=2, concat_axis=2, til...]
  transfers between devices with their start and end apart: 5 -> 0, of which waited for: 4 -> 0; matrix products, arithmetic and copies ran while one was open for 4% -> 0% of each run, Pallas kernels for 0% -> 0%
where the time goes in v1:
time: 83.3 us; the launch traced here: 82.8 us
  Pallas kernels  70.1 us (84%)
  local copies, waits for them, and re-layouts  12 us (14%)
    pallas_call x1, Pallas kernels, body(): pl.pallas_call(kernel, out_shape=(jax.ShapeDtypeStruct((LEVELS, width), F...  70.1 us
    unnamed x30, local copies, waits for them, and re-layouts  12 us

profile of v1, /device:TPU:6, one launch (start us, length us, event | category | flops | bytes accessed | tf_op | source)
XLA Modules:
  0.0 82.8 jit_solution(15100143730455178053)
XLA Ops:
  0.6 0.0 copy-start
  0.6 1.3 %copy-done = f32[7,24,2048]{2,1,0:T(8,128)S(1)} copy-done((f32[7,24,2048]{2,1,0:T(8,128)S(1)}, f32[7,24,2048]{2,1,0:T(8,128)}, u32[]{:S(2)}) %copy-start) | copy-done | bytes 1376280
  2.0 0.0 copy-start.1
  2.0 1.0 %copy-done.1 = f32[2,24,2048]{2,1,0:T(8,128)S(1)} copy-done((f32[2,24,2048]{2,1,0:T(8,128)S(1)}, f32[2,24,2048]{2,1,0:T(8,128)}, u32[]{:S(2)}) %copy-start.1) | copy-done | bytes 393240
  3.0 0.0 copy-start.2
  3.0 0.9 %copy-done.2 = f32[24,2048]{1,0:T(8,128)S(1)} copy-done((f32[24,2048]{1,0:T(8,128)S(1)}, f32[24,2048]{1,0:T(8,128)}, u32[]{:S(2)}) %copy-start.2) | copy-done | bytes 196632
  3.9 0.0 copy-start.3
  3.9 0.7 copy-done.3
  4.6 0.0 copy-start.4
  4.6 0.7 copy-done.4
  5.3 0.0 copy-start.5
  5.3 0.7 copy-done.5
  6.0 0.0 copy-start.6
  6.0 0.7 copy-done.6
  6.7 0.0 copy-start.7
  6.7 0.7 copy-done.7
  7.4 0.0 copy-start.8
  7.4 0.7 copy-done.8
  8.1 0.0 copy-start.9
  8.1 0.7 copy-done.9
  8.8 0.0 copy-start.10
  8.8 0.7 copy-done.10
  9.4 0.0 copy-start.11
  9.4 0.7 copy-done.11
  10.1 0.0 copy-start.12
  10.1 0.7 copy-done.12
  10.7 0.0 copy-start.13
  10.7 0.7 copy-done.13
  11.4 70.1 %shard_map.149 = (f32[24,2048]{1,0:T(8,128)S(1)}, f32[16,128]{1,0:T(8,128)S(1)}) custom-call(f32[168,2048]{1,0:T(8,128)S(1)} %bitcast.11, f32[24,2048]{1,0:T(8,128)S(1)} %copy-done.2, f32[48,2048]{1,0:T(8,128)S(1)} %bitcast.12, s32[16,128]{1,0:T(8,128)S(1)} %bitcast.13, f32[16,128]{1,0:T(8,128)S(1)} %bitcast.14, f32[16,128]{1,0:T(8,128)S(1)} %bitcast.15, ...), custom_call_target="tpu_custom_call" | custom-call | tf_op jit(solution)/shard_map/pallas_call | solution.py:385
  81.5 0.7 copy.18
  82.2 0.6 copy.19
Async XLA Ops:
  0.6 1.3 %copy-start = (f32[7,24,2048]{2,1,0:T(8,128)S(1)}, f32[7,24,2048]{2,1,0:T(8,128)}, u32[]{:S(2)}) copy-start(f32[7,24,2048]{2,1,0:T(8,128)} %param.14) | copy-start | bytes 4128772
  2.0 1.0 %copy-start.1 = (f32[2,24,2048]{2,1,0:T(8,128)S(1)}, f32[2,24,2048]{2,1,0:T(8,128)}, u32[]{:S(2)}) copy-start(f32[2,24,2048]{2,1,0:T(8,128)} %param.16) | copy-start | bytes 1179652
  3.0 0.9 %copy-start.2 = (f32[24,2048]{1,0:T(8,128)S(1)}, f32[24,2048]{1,0:T(8,128)}, u32[]{:S(2)}) copy-start(f32[24,2048]{1,0:T(8,128)} %mass_ref.1) | copy-start | bytes 589828
  3.9 0.7 copy-start.3
  4.6 0.7 copy-start.4
  5.3 0.7 copy-start.5
  6.0 0.7 copy-start.6
  6.7 0.7 copy-start.7
  7.4 0.7 copy-start.8
  8.1 0.7 copy-start.9
  8.8 0.7 copy-start.10
  9.4 0.7 copy-start.11
  10.1 0.7 copy-start.12
  10.7 0.7 copy-start.13

commit v2 on v1

v2 whole, which is shorter than its diff:
```python
import functools

import jax
import jax.numpy as jnp
from jax import lax
from jax.experimental import pallas as pl
from jax.experimental.pallas import tpu as pltpu
from jax.sharding import PartitionSpec as P

WATER_SSA = 0.999
ICE_SSA = 0.99
WATER_ASYM = 0.85
ICE_ASYM = 0.78
DIFFUSIVITY = 1.66
LOG2E = 1.4426950408889634

F32 = jnp.float32
BF16 = jnp.bfloat16
LANES = 128
HALF = 64
GPTS = 112
BANDS = 14
LEVELS = 24
GASES = 7
FIELD_ROWS = 8 * LEVELS
CLOUD_ROWS = 2 * LEVELS
STATE_ROWS = 56
PACKED_ROWS = 32
LIT_ROW = 20
STEPS = 8
TILES = 16
UNROLL = 24
MESH = pl.DeviceIdType.MESH
SPACE = pltpu.HBM


def split3(x):
    first = x.astype(BF16).astype(F32)
    rest = x - first
    second = rest.astype(BF16).astype(F32)
    return first, second, rest - second


def lane_pad(x):
    return jnp.concatenate([x, jnp.zeros((x.shape[0], LANES - x.shape[1]), F32)], 1)


def make_tables(gas, ray, cloud, solar, surface, snow, coef_ref, solar_ref, albtab_ref):
    shape = (BANDS, LANES)
    band = lax.broadcasted_iota(jnp.int32, shape, 1) // 8 == lax.broadcasted_iota(jnp.int32, shape, 0)
    cloud_gpt = jnp.dot(
        cloud, band.astype(F32), precision=lax.Precision.HIGHEST, preferred_element_type=F32
    )
    ray = lane_pad(ray)
    water, ice = WATER_SSA * cloud_gpt[0:1], ICE_SSA * cloud_gpt[1:2]
    zero6, zero7, zero32 = (jnp.zeros((n, LANES), F32) for n in (6, 7, 32))
    stacks = (
        [lane_pad(gas), ray, cloud_gpt, zero6],
        [zero7, 0.5 * ray, 0.5 * (1 - WATER_ASYM) * water, 0.5 * (1 - ICE_ASYM) * ice, zero6],
        [zero7, 0.5 * ray, 0.5 * (1 + WATER_ASYM) * water, 0.5 * (1 + ICE_ASYM) * ice, zero6],
    )
    for index, stack in enumerate(stacks):
        a1, a2, a3 = split3(jnp.concatenate(stack, 0))
        terms = jnp.concatenate([a1, a1, a2, a1, a3, a2, zero32], 0)
        coef_ref[pl.ds(index * GPTS, GPTS), :] = jnp.transpose(terms)[:GPTS].astype(BF16)
    solar = lane_pad(solar)
    solar = solar / jnp.sum(solar)
    square = (LANES, LANES)
    solar_ref[...] = jnp.transpose(jnp.broadcast_to(solar, square))[:GPTS]
    rows = jnp.concatenate([lane_pad(surface), lane_pad(snow)], 0)
    for index in range(5):
        albtab_ref[pl.ds(index * 16, 16), :] = jnp.transpose(
            jnp.broadcast_to(rows[index : index + 1], square)
        )[:16]


def compute_tile(x_ref, state, coef_ref, solar_ref, albtab_ref, alb_ref, layer_ref, net_ref):
    block = (8, LANES)
    kind, share, age, cosine = state[0:1], state[1:2], state[2:3], state[3:4]
    beam_scale = jnp.broadcast_to(-LOG2E / cosine, block)
    base = jnp.zeros((16, LANES), F32)
    for index in range(4):
        base = jnp.where(kind == float(index), albtab_ref[pl.ds(index * 16, 16), :], base)
    fresh = albtab_ref[pl.ds(64, 16), :] * (1.0 - 0.5 * age)
    alb_ref[...] = (1.0 - share) * base + share * fresh

    def upward(step, carried):
        alb, src = carried
        layer = LEVELS - 1 - step
        x1, x2, x3 = split3(x_ref[pl.ds(layer, 16, stride=LEVELS), :])
        terms = jnp.concatenate([x1, x2, x1, x3, x1, x2, jnp.zeros((32, LANES), F32)], 0)
        optics = jnp.dot(coef_ref[...], terms.astype(BF16), preferred_element_type=F32)
        next_alb, next_src = [], []
        for b in range(BANDS):
            depth = optics[8 * b : 8 * b + 8]
            inv_depth = pl.reciprocal(depth, approx=True)
            backward = optics[GPTS + 8 * b : GPTS + 8 * b + 8] * inv_depth
            onward = optics[2 * GPTS + 8 * b : 2 * GPTS + 8 * b + 8] * inv_depth
            diffuse_exp = jnp.exp2(depth * (-DIFFUSIVITY * LOG2E))
            beam_exp = jnp.exp2(depth * beam_scale)
            diffuse_loss = 1.0 - diffuse_exp
            beam_loss = 1.0 - beam_exp
            refl_diff = backward * diffuse_loss
            tran_diff = diffuse_exp + onward * diffuse_loss
            refl_dir = backward * beam_loss
            scat_dir = onward * beam_loss
            denom = pl.reciprocal(1.0 - refl_diff * alb[b], approx=True)
            through = tran_diff * denom
            src_beam = src[b] * beam_exp
            gain = (refl_diff * src_beam + scat_dir) * denom
            src_here = refl_dir + through * (src_beam + alb[b] * scat_dir)
            alb_here = refl_diff + tran_diff * through * alb[b]
            layer_ref[layer, 0, b] = through
            layer_ref[layer, 1, b] = gain
            layer_ref[layer, 2, b] = beam_exp
            layer_ref[layer, 3, b] = 1.0 - alb_here
            layer_ref[layer, 4, b] = 1.0 - src_here
            next_alb.append(alb_here)
            next_src.append(src_here)
        return tuple(next_alb), tuple(next_src)

    ground = tuple(jnp.broadcast_to(alb_ref[b : b + 1, :], block) for b in range(BANDS))
    lax.fori_loop(0, LEVELS, upward, (ground, ground), unroll=UNROLL)

    def downward(layer, carried):
        down, direct = carried
        net = jnp.zeros(block, F32)
        next_down, next_direct = [], []
        for b in range(BANDS):
            net = net + (layer_ref[layer, 3, b] * down[b] + layer_ref[layer, 4, b] * direct[b])
            next_down.append(layer_ref[layer, 0, b] * down[b] + layer_ref[layer, 1, b] * direct[b])
            next_direct.append(layer_ref[layer, 2, b] * direct[b])
        net_ref[layer] = net
        return tuple(next_down), tuple(next_direct)

    beam = tuple(solar_ref[pl.ds(8 * b, 8), :] * cosine for b in range(BANDS))
    none = tuple(jnp.zeros(block, F32) for b in range(BANDS))
    down, direct = lax.fori_loop(0, LEVELS, downward, (none, beam), unroll=UNROLL)
    net = jnp.zeros(block, F32)
    for b in range(BANDS):
        net = net + (1.0 - jnp.broadcast_to(alb_ref[b : b + 1, :], block)) * (down[b] + direct[b])
    net_ref[LEVELS] = net
    nets = jnp.sum(net_ref[...], axis=1)
    mass = x_ref[pl.ds(GASES * LEVELS, LEVELS), :]
    return float(LEVELS) * (nets[:LEVELS] - nets[1:]) / mass, nets[LEVELS:]


def kernel(
    gas_hbm, mass_hbm, cloud_hbm, kind_hbm, cover_hbm, age_hbm, cosine_hbm, lit_hbm,
    coeff_hbm, ray_hbm, cext_hbm, surface_hbm, snow_hbm, weight_hbm,
    heat_ref, flux_ref,
    gas_own, mass_own, cloud_ref, kind_ref, cover_ref, age_ref, cosine_ref, lit_ref,
    coeff_ref, ray_ref, cext_ref, surface_ref, snow_ref, weight_ref,
    gas_in, mass_in, send, recv, heat_out, flux_out, flux_in,
    x_ref, coef_ref, solar_ref, albtab_ref, alb_ref, layer_ref, net_ref,
    load_sem, own_sem, gas_send, gas_recv, mass_send, mass_recv,
    state_send, state_recv, heat_send, heat_recv, flux_send, flux_recv,
):
    pair, elem = lax.axis_index("pair"), lax.axis_index("elem")
    half_pairs = lax.axis_size("pair") // 2
    side, group = pair // half_pairs, pair % half_pairs
    z, y = elem // 4, elem % 4
    z_block, z_odd, y_pair, y_low = z // 2, z % 2, y // 2, y % 2
    other = 1 - side

    def device(which_side, which_elem):
        return (which_side * half_pairs + group, which_elem)

    partner = device(other, elem)

    def columns(tile):
        return pl.ds(pl.multiple_of(tile * LANES, LANES), LANES)

    def step_tile(step, which_side):
        return 2 * (2 * ((z_block + step // 2) % 4) + which_side) + (y_pair + step % 2) % 2

    def own_copies(step):
        tile = columns(step_tile(step, side))
        return (
            pltpu.make_async_copy(gas_hbm.at[:, tile], gas_own.at[step], own_sem.at[0, step]),
            pltpu.make_async_copy(mass_hbm.at[:, tile], mass_own.at[step], own_sem.at[1, step]),
        )

    state_loads = [
        pltpu.make_async_copy(source, target, load_sem.at[index])
        for index, (source, target) in enumerate((
            (cloud_hbm, cloud_ref), (kind_hbm, kind_ref), (cover_hbm, cover_ref),
            (age_hbm, age_ref), (cosine_hbm, cosine_ref), (lit_hbm, lit_ref),
        ))
    ]
    table_loads = [
        pltpu.make_async_copy(source, target, load_sem.at[6 + index])
        for index, (source, target) in enumerate((
            (coeff_hbm, coeff_ref), (ray_hbm, ray_ref), (cext_hbm, cext_ref),
            (surface_hbm, surface_ref), (snow_hbm, snow_ref), (weight_hbm, weight_ref),
        ))
    ]

    barrier = pltpu.get_barrier_semaphore()

    def greet(which_side, k):
        @pl.when(jnp.logical_or(which_side != side, k != elem))
        def _():
            pl.semaphore_signal(barrier, inc=1, device_id=device(which_side, k), device_id_type=MESH)

    def greet_all(k, _):
        greet(z_odd, k)
        return 0

    def greet_some(index, _):
        greet(1 - z_odd, (2 * (index // 4) + side) * 4 + index % 4)
        return 0

    lax.fori_loop(0, 32, greet_all, 0)
    lax.fori_loop(0, 16, greet_some, 0)

    for copy in state_loads + table_loads:
        copy.start()

    def load_own(step, _):
        for copy in own_copies(step):
            copy.start()
        return 0

    lax.fori_loop(0, STEPS, load_own, 0)

    low_packed = lax.broadcasted_iota(jnp.int32, (PACKED_ROWS, LANES), 1) < HALF
    low8 = lax.broadcasted_iota(jnp.int32, (8, LANES), 1) < HALF

    for copy in state_loads:
        copy.wait()

    for tile in range(TILES):
        row = slice(tile, tile + 1)
        kind = kind_ref[row, :]
        share = jnp.where(kind >= 1, cover_ref[row, :], 0.0)
        first = cloud_ref[0:PACKED_ROWS, tile * LANES : (tile + 1) * LANES]
        second = jnp.concatenate(
            [
                cloud_ref[PACKED_ROWS:CLOUD_ROWS, tile * LANES : (tile + 1) * LANES],
                kind.astype(F32), share, age_ref[row, :], cosine_ref[row, :], lit_ref[row, :].astype(F32),
                jnp.zeros((11, LANES), F32),
            ],
            0,
        )
        send[2 * tile] = jnp.where(low_packed, first, pltpu.roll(second, HALF, 1))
        send[2 * tile + 1] = jnp.where(low_packed, pltpu.roll(first, HALF, 1), second)

    for copy in table_loads:
        copy.wait()
    make_tables(
        coeff_ref[...], ray_ref[...], cext_ref[...], weight_ref[...], surface_ref[...], snow_ref[...],
        coef_ref, solar_ref, albtab_ref,
    )
    x_ref[...] = jnp.zeros_like(x_ref)

    pl.semaphore_wait(barrier, 48 - jnp.where(side == z_odd, 1, 0))

    def gas_copies(step):
        tile = columns(step_tile(step, other))
        return (
            pltpu.make_async_remote_copy(
                src_ref=gas_hbm.at[:, tile], dst_ref=gas_in.at[step],
                send_sem=gas_send.at[step], recv_sem=gas_recv.at[step],
                device_id=partner, device_id_type=MESH,
            ),
            pltpu.make_async_remote_copy(
                src_ref=mass_hbm.at[:, tile], dst_ref=mass_in.at[step],
                send_sem=mass_send.at[step], recv_sem=mass_recv.at[step],
                device_id=partner, device_id_type=MESH,
            ),
        )

    def for_states(step, remote, local=None):
        for z_low in range(2):
            z_to = 2 * ((z_block + 4 - step // 2) % 4) + z_low
            for low in range(2):
                k = 4 * z_to + 2 * ((y_pair + step % 2) % 2) + low
                here = jnp.logical_and(z_odd == side, k == elem)

                @pl.when(jnp.logical_not(here))
                def _():
                    remote(
                        pltpu.make_async_remote_copy(
                            src_ref=send.at[k], dst_ref=recv.at[side, step, y_low],
                            send_sem=state_send.at[k], recv_sem=state_recv.at[side, step, y_low],
                            device_id=device(z_odd, k), device_id_type=MESH,
                        )
                    )

                if local is not None:
                    @pl.when(here)
                    def _():
                        local(
                            pltpu.make_async_copy(
                                send.at[k], recv.at[side, step, y_low], state_recv.at[side, step, y_low]
                            )
                        )

    def send_step(step, _):
        for copy in gas_copies(step):
            copy.start()
        for_states(step, lambda copy: copy.start(), lambda copy: copy.start())
        return 0

    lax.fori_loop(0, STEPS, send_step, 0)

    def heat_copy(step):
        return pltpu.make_async_remote_copy(
            src_ref=heat_out.at[step], dst_ref=heat_ref.at[:, columns(step_tile(step, side))],
            send_sem=heat_send.at[step], recv_sem=heat_recv.at[step],
            device_id=partner, device_id_type=MESH,
        )

    def for_fluxes(step, remote, local=None):
        for which_side in range(2):
            for low in range(2):
                k = 2 * step_tile(step, side) + low
                source = flux_out.at[step, which_side, (low + y_low) % 2]
                here = jnp.logical_and(which_side == side, k == elem)

                @pl.when(jnp.logical_not(here))
                def _():
                    remote(
                        pltpu.make_async_remote_copy(
                            src_ref=source, dst_ref=flux_in.at[elem],
                            send_sem=flux_send.at[step, which_side, low], recv_sem=flux_recv.at[elem],
                            device_id=device(which_side, k), device_id_type=MESH,
                        )
                    )

                if local is not None:
                    @pl.when(here)
                    def _():
                        local(pltpu.make_async_copy(source, flux_in.at[elem], flux_recv.at[elem]))

    def one_tile(step, _):
        for copy in own_copies(step):
            copy.wait()
        for which_side in range(2):
            for low in range(2):
                block = recv.at[which_side, step, low]
                pltpu.make_async_copy(block, block, state_recv.at[which_side, step, low]).wait()
        for copy in gas_copies(step):
            copy.wait_recv()
        own0, own1 = recv[side, step, 0], recv[side, step, 1]
        other0, other1 = recv[other, step, 0], recv[other, step, 1]

        def lit_masks(block0, block1):
            row0, row1 = block0[16:24], block1[16:24]
            turned0, turned1 = pltpu.roll(row0, HALF, 1), pltpu.roll(row1, HALF, 1)
            at = slice(LIT_ROW - 16, LIT_ROW - 15)
            return (
                jnp.where(low8, turned0, row0)[at] > 0.5,
                jnp.where(low8, turned1, row1)[at] > 0.5,
                jnp.where(low8, turned0, row1)[at] > 0.5,
            )

        mask0, mask1, own_lit = lit_masks(own0, own1)
        other_lit = lit_masks(other0, other1)[2]
        part0 = jnp.where(mask0, own0, other0)
        part1 = jnp.where(mask1, own1, other1)
        first = jnp.where(low_packed, part0, pltpu.roll(part1, HALF, 1))
        second = jnp.where(low_packed, pltpu.roll(part0, HALF, 1), part1)
        gas_rows = GASES * LEVELS
        x_ref[pl.ds(0, gas_rows), :] = jnp.where(own_lit, gas_own[step], gas_in[step])
        x_ref[pl.ds(gas_rows, LEVELS), :] = jnp.where(own_lit, mass_own[step], mass_in[step])
        x_ref[pl.ds(FIELD_ROWS, PACKED_ROWS), :] = first
        x_ref[pl.ds(FIELD_ROWS + PACKED_ROWS, CLOUD_ROWS - PACKED_ROWS), :] = second[0 : CLOUD_ROWS - PACKED_ROWS]
        heat, flux = compute_tile(
            x_ref, second[16:24], coef_ref, solar_ref, albtab_ref, alb_ref, layer_ref, net_ref
        )
        heat_out[step] = jnp.where(other_lit, heat, 0.0)
        heat_copy(step).start()
        for which_side in range(2):
            lit = jnp.where(which_side == side, own_lit.astype(F32), other_lit.astype(F32)) > 0.5
            kept = jnp.broadcast_to(jnp.where(lit, flux, 0.0), (8, LANES))
            flux_out[step, which_side, 0] = kept[0:1]
            flux_out[step, which_side, 1] = pltpu.roll(kept, HALF, 1)[0:1]
        for_fluxes(step, lambda copy: copy.start(), lambda copy: copy.start())
        heat_ref[:, columns(step_tile(step, side))] = jnp.where(own_lit, heat, 0.0)
        return 0

    lax.fori_loop(0, STEPS, one_tile, 0)

    def finish(step, _):
        for copy in gas_copies(step):
            copy.wait_send()
        for_states(step, lambda copy: copy.wait_send())
        for_fluxes(step, lambda copy: copy.wait_send())
        heat_copy(step).wait()
        return 0

    def finish_flux(tile, _):
        for low in range(2):
            row = flux_in.at[2 * tile + low]
            pltpu.make_async_copy(row, row, flux_recv.at[2 * tile + low]).wait()
        flux_ref[pl.ds(tile, 1), :] = jnp.where(low8[0:1], flux_in[2 * tile], flux_in[2 * tile + 1])
        return 0

    lax.fori_loop(0, STEPS, finish, 0)
    lax.fori_loop(0, TILES, finish_flux, 0)


def body(
    gas_amounts, layer_mass, cloud_paths, surface_kind, snow_cover, snow_age, cos_zenith, sunlit,
    gas_coeff, rayleigh, cloud_ext, surface_table, snow_table, solar_weight,
):
    width = layer_mass.shape[1]
    rows = lambda x: x.reshape(width // LANES, LANES)
    dma = pltpu.SemaphoreType.DMA
    hbm = pl.BlockSpec(memory_space=SPACE)
    vmem = pl.BlockSpec(memory_space=pltpu.VMEM)
    wide = lambda *lead: pltpu.VMEM(lead + (LANES,), F32)
    heating, flux = pl.pallas_call(
        kernel,
        out_shape=(
            jax.ShapeDtypeStruct((LEVELS, width), F32),
            jax.ShapeDtypeStruct((width // LANES, LANES), F32),
        ),
        in_specs=[hbm] * 14,
        out_specs=(vmem, vmem),
        scratch_shapes=[
            wide(STEPS, GASES * LEVELS), wide(STEPS, LEVELS), pltpu.VMEM((CLOUD_ROWS, width), F32),
            pltpu.VMEM((TILES, LANES), jnp.int32), wide(TILES), wide(TILES), wide(TILES),
            pltpu.VMEM((TILES, LANES), jnp.int32),
            pltpu.VMEM((GASES, GPTS), F32), pltpu.VMEM((1, GPTS), F32), pltpu.VMEM((2, BANDS), F32),
            pltpu.VMEM((4, BANDS), F32), pltpu.VMEM((1, BANDS), F32), pltpu.VMEM((1, GPTS), F32),
            wide(STEPS, GASES * LEVELS), wide(STEPS, LEVELS),
            wide(32, PACKED_ROWS), wide(2, STEPS, 2, PACKED_ROWS),
            wide(STEPS, LEVELS), wide(STEPS, 2, 2, 1), wide(32, 1),
            wide(16 * LEVELS), pltpu.VMEM((3 * GPTS, LANES), BF16), wide(GPTS), wide(80), wide(16),
            wide(LEVELS, 5, BANDS, 8), wide(LEVELS + 1, 8),
            dma((12,)), dma((2, STEPS)), dma((STEPS,)), dma((STEPS,)), dma((STEPS,)), dma((STEPS,)),
            dma((32,)), dma((2, STEPS, 2)), dma((STEPS,)), dma((STEPS,)), dma((STEPS, 2, 2)), dma((32,)),
        ],
        compiler_params=pltpu.CompilerParams(
            collective_id=0, has_side_effects=True, vmem_limit_bytes=60 * 2**20
        ),
    )(
        gas_amounts.reshape(GASES * LEVELS, width),
        layer_mass,
        cloud_paths.reshape(CLOUD_ROWS, width),
        rows(surface_kind), rows(snow_cover), rows(snow_age), rows(cos_zenith), rows(sunlit),
        gas_coeff, rayleigh.reshape(1, GPTS), cloud_ext, surface_table,
        snow_table.reshape(1, BANDS), solar_weight.reshape(1, GPTS),
    )
    return heating, flux.reshape(width)


def solution(mesh):
    columns = ("pair", "elem")
    placed = (
        P(None, None, columns), P(None, columns), P(None, None, columns),
        P(columns), P(columns), P(columns), P(columns), P(columns),
        P(), P(), P(), P(), P(), P(),
    )
    return jax.shard_map(
        body,
        mesh=mesh,
        in_specs=placed,
        out_specs=(P(None, columns), P(columns)),
        check_vma=False,
    )
```

time: 83.3 us -> 55.1 us (0.66)
  Pallas kernels: 70.1 us -> 51.4 us
  local copies, waits for them, and re-layouts: 12 us -> 2.91 us
    pallas_call x1, Pallas kernels: 70.1 us -> 51.4 us  [body(): pl.pallas_call(kernel, out_shape=(jax.ShapeDtypeStruct((LEVELS, width), F...]
    unnamed x30 -> x2, local copies, waits for them, and re-layouts: 12 us -> 2.91 us
where the time goes in v2:
time: 55.1 us; the launch traced here: 54.9 us
  Pallas kernels  51.4 us (93%)
  local copies, waits for them, and re-layouts  2.91 us (5%)
  between operations  0.64 us (1%)
    pallas_call x1, Pallas kernels, body(): pl.pallas_call(kernel, out_shape=(jax.ShapeDtypeStruct((LEVELS, width), F...  51.4 us
    unnamed x2, local copies, waits for them, and re-layouts  2.91 us

profile of v2, /device:TPU:6, one launch (start us, length us, event | category | flops | bytes accessed | tf_op | source)
XLA Modules:
  0.0 54.9 jit_solution(5517823520794829458)
XLA Ops:
  0.6 51.4 %shard_map.149 = (f32[24,2048]{1,0:T(8,128)}, f32[16,128]{1,0:T(8,128)}) custom-call(f32[168,2048]{1,0:T(8,128)} %bitcast.11, f32[24,2048]{1,0:T(8,128)} %mass_hbm.1, f32[48,2048]{1,0:T(8,128)} %bitcast.12, s32[16,128]{1,0:T(8,128)} %bitcast.13, f32[16,128]{1,0:T(8,128)} %bitcast.14, f32[16,128]{1,0:T(8,128)} %bitcast.15, f32[16,128]{1,0:T(8,128)} %bitcast.16, ...), custom_call_target="tpu_custom_call" | custom-call | tf_op jit(solution)/shard_map/pallas_call | solution.py:415
  52.0 1.6 %copy.18 = f32[24,2048]{1,0:T(8,128)} copy(f32[24,2048]{1,0:T(8,128)} %get-tuple-element.8) | data formatting | bytes 393216
  53.6 1.3 %copy.19 = f32[2048]{0:T(1024)} copy(f32[2048]{0:T(1024)} %bitcast.18) | data formatting | bytes 16384

commit v3 on v2

v3 whole, which is shorter than its diff:
```python
import functools

import jax
import jax.numpy as jnp
from jax import lax
from jax.experimental import pallas as pl
from jax.experimental.pallas import tpu as pltpu
from jax.sharding import PartitionSpec as P

WATER_SSA = 0.999
ICE_SSA = 0.99
WATER_ASYM = 0.85
ICE_ASYM = 0.78
DIFFUSIVITY = 1.66
LOG2E = 1.4426950408889634

F32 = jnp.float32
BF16 = jnp.bfloat16
LANES = 128
HALF = 64
GPTS = 112
BANDS = 14
LEVELS = 24
GASES = 7
FIELD_ROWS = 8 * LEVELS
CLOUD_ROWS = 2 * LEVELS
GAS_ROWS = GASES * LEVELS
PACKED_ROWS = 32
SENT_ROWS = 28
AHEAD = 3
STEPS = 8
TILES = 16
UNROLL = 24
MESH = pl.DeviceIdType.MESH
SPACE = pltpu.HBM


def split3(x):
    first = x.astype(BF16).astype(F32)
    rest = x - first
    second = rest.astype(BF16).astype(F32)
    return first, second, rest - second


def lane_pad(x):
    return jnp.concatenate([x, jnp.zeros((x.shape[0], LANES - x.shape[1]), F32)], 1)


def make_tables(gas, ray, cloud, solar, surface, snow, coef_ref, solar_ref, albtab_ref):
    shape = (BANDS, LANES)
    band = lax.broadcasted_iota(jnp.int32, shape, 1) // 8 == lax.broadcasted_iota(jnp.int32, shape, 0)
    cloud_gpt = jnp.dot(
        cloud, band.astype(F32), precision=lax.Precision.HIGHEST, preferred_element_type=F32
    )
    ray = lane_pad(ray)
    water, ice = WATER_SSA * cloud_gpt[0:1], ICE_SSA * cloud_gpt[1:2]
    zero6, zero7, zero32 = (jnp.zeros((n, LANES), F32) for n in (6, 7, 32))
    stacks = (
        [lane_pad(gas), ray, cloud_gpt, zero6],
        [zero7, 0.5 * ray, 0.5 * (1 - WATER_ASYM) * water, 0.5 * (1 - ICE_ASYM) * ice, zero6],
        [zero7, 0.5 * ray, 0.5 * (1 + WATER_ASYM) * water, 0.5 * (1 + ICE_ASYM) * ice, zero6],
    )
    for index, stack in enumerate(stacks):
        a1, a2, a3 = split3(jnp.concatenate(stack, 0) * (-DIFFUSIVITY * LOG2E))
        terms = jnp.concatenate([a1, a1, a2, a1, a3, a2, zero32], 0)
        coef_ref[pl.ds(index * GPTS, GPTS), :] = jnp.transpose(terms)[:GPTS].astype(BF16)
    solar = lane_pad(solar)
    solar = solar / jnp.sum(solar)
    square = (LANES, LANES)
    solar_ref[...] = jnp.transpose(jnp.broadcast_to(solar, square))[:GPTS]
    rows = jnp.concatenate([lane_pad(surface), lane_pad(snow)], 0)
    for index in range(5):
        albtab_ref[pl.ds(index * 16, 16), :] = jnp.transpose(
            jnp.broadcast_to(rows[index : index + 1], square)
        )[:16]


def compute_tile(x_ref, state, coef_ref, solar_ref, albtab_ref, alb_ref, layer_ref, net_ref):
    block = (8, LANES)
    kind, share, age, cosine = state[0:1], state[1:2], state[2:3], state[3:4]
    beam_scale = jnp.broadcast_to((1.0 / DIFFUSIVITY) / cosine, block)
    base = jnp.zeros((16, LANES), F32)
    for index in range(4):
        base = jnp.where(kind == float(index), albtab_ref[pl.ds(index * 16, 16), :], base)
    fresh = albtab_ref[pl.ds(64, 16), :] * (1.0 - 0.5 * age)
    alb_ref[...] = (1.0 - share) * base + share * fresh

    def upward(step, carried):
        alb, src = carried
        layer = LEVELS - 1 - step
        x1, x2, x3 = split3(x_ref[pl.ds(layer, 16, stride=LEVELS), :])
        terms = jnp.concatenate([x1, x2, x1, x3, x1, x2, jnp.zeros((32, LANES), F32)], 0)
        optics = jnp.dot(coef_ref[...], terms.astype(BF16), preferred_element_type=F32)
        next_alb, next_src = [], []
        for b in range(BANDS):
            depth = optics[8 * b : 8 * b + 8]
            inv_depth = pl.reciprocal(depth, approx=True)
            backward = optics[GPTS + 8 * b : GPTS + 8 * b + 8] * inv_depth
            onward = optics[2 * GPTS + 8 * b : 2 * GPTS + 8 * b + 8] * inv_depth
            diffuse_exp = jnp.exp2(depth)
            beam_exp = jnp.exp2(depth * beam_scale)
            diffuse_loss = 1.0 - diffuse_exp
            beam_loss = 1.0 - beam_exp
            refl_diff = backward * diffuse_loss
            tran_diff = diffuse_exp + onward * diffuse_loss
            refl_dir = backward * beam_loss
            scat_dir = onward * beam_loss
            denom = pl.reciprocal(1.0 - refl_diff * alb[b], approx=True)
            through = tran_diff * denom
            src_beam = src[b] * beam_exp
            gain = (refl_diff * src_beam + scat_dir) * denom
            src_here = refl_dir + through * (src_beam + alb[b] * scat_dir)
            alb_here = refl_diff + tran_diff * through * alb[b]
            layer_ref[layer, 0, b] = through
            layer_ref[layer, 1, b] = gain
            layer_ref[layer, 2, b] = beam_exp
            layer_ref[layer, 3, b] = 1.0 - alb_here
            layer_ref[layer, 4, b] = 1.0 - src_here
            next_alb.append(alb_here)
            next_src.append(src_here)
        return tuple(next_alb), tuple(next_src)

    ground = tuple(jnp.broadcast_to(alb_ref[b : b + 1, :], block) for b in range(BANDS))
    lax.fori_loop(0, LEVELS, upward, (ground, ground), unroll=UNROLL)

    def downward(layer, carried):
        down, direct = carried
        nets, next_down, next_direct = [], [], []
        for b in range(BANDS):
            nets.append(layer_ref[layer, 3, b] * down[b] + layer_ref[layer, 4, b] * direct[b])
            next_down.append(layer_ref[layer, 0, b] * down[b] + layer_ref[layer, 1, b] * direct[b])
            next_direct.append(layer_ref[layer, 2, b] * direct[b])
        while len(nets) > 1:
            nets = [sum(nets[i : i + 2][1:], nets[i]) for i in range(0, len(nets), 2)]
        net_ref[layer] = nets[0]
        return tuple(next_down), tuple(next_direct)

    beam = tuple(solar_ref[pl.ds(8 * b, 8), :] * cosine for b in range(BANDS))
    none = tuple(jnp.zeros(block, F32) for b in range(BANDS))
    down, direct = lax.fori_loop(0, LEVELS, downward, (none, beam), unroll=UNROLL)
    net = jnp.zeros(block, F32)
    for b in range(BANDS):
        net = net + (1.0 - jnp.broadcast_to(alb_ref[b : b + 1, :], block)) * (down[b] + direct[b])
    net_ref[LEVELS] = net
    nets = jnp.sum(net_ref[...], axis=1)
    mass = x_ref[pl.ds(GASES * LEVELS, LEVELS), :]
    return float(LEVELS) * (nets[:LEVELS] - nets[1:]) / mass, nets[LEVELS:]


def kernel(
    gas_hbm, mass_hbm, cloud_hbm, kind_hbm, cover_hbm, age_hbm, cosine_hbm, lit_hbm,
    coeff_hbm, ray_hbm, cext_hbm, surface_hbm, snow_hbm, weight_hbm,
    heat_ref, flux_ref,
    gas_own, cloud_ref, kind_ref, cover_ref, age_ref, cosine_ref, lit_ref,
    coeff_ref, ray_ref, cext_ref, surface_ref, snow_ref, weight_ref,
    gas_in, send, recv, heat_out, flux_out, flux_in,
    x_ref, coef_ref, solar_ref, albtab_ref, alb_ref, layer_ref, net_ref,
    load_sem, own_sem, gas_send, gas_recv,
    state_send, state_recv, heat_send, heat_recv, flux_send, flux_recv,
):
    pair, elem = lax.axis_index("pair"), lax.axis_index("elem")
    half_pairs = lax.axis_size("pair") // 2
    side, group = pair // half_pairs, pair % half_pairs
    z, y = elem // 4, elem % 4
    z_block, z_odd, y_pair, y_low = z // 2, z % 2, y // 2, y % 2
    other = 1 - side
    some_local = z_odd == side

    def device(which_side, which_elem):
        return (which_side * half_pairs + group, which_elem)

    partner = device(other, elem)

    def columns(tile):
        return pl.ds(pl.multiple_of(tile * LANES, LANES), LANES)

    def wait_bytes(ref, sem):
        pltpu.make_async_copy(ref, ref, sem).wait()

    def step_tile(step, which_side):
        return 2 * (2 * ((z_block + step // 2) % 4) + which_side) + (y_pair + step % 2) % 2

    state_loads = [
        pltpu.make_async_copy(source, target, load_sem.at[index])
        for index, (source, target) in enumerate((
            (cloud_hbm, cloud_ref), (kind_hbm, kind_ref), (cover_hbm, cover_ref),
            (age_hbm, age_ref), (cosine_hbm, cosine_ref), (lit_hbm, lit_ref),
        ))
    ]
    table_loads = [
        pltpu.make_async_copy(source, target, load_sem.at[6 + index])
        for index, (source, target) in enumerate((
            (coeff_hbm, coeff_ref), (ray_hbm, ray_ref), (cext_hbm, cext_ref),
            (surface_hbm, surface_ref), (snow_hbm, snow_ref), (weight_hbm, weight_ref),
        ))
    ]
    for copy in state_loads:
        copy.start()

    barrier = pltpu.get_barrier_semaphore()

    def greet(which_side, k):
        @pl.when(jnp.logical_or(which_side != side, k != elem))
        def _():
            pl.semaphore_signal(barrier, inc=1, device_id=device(which_side, k), device_id_type=MESH)

    def greet_all(k, _):
        greet(z_odd, k)
        return 0

    def greet_some(index, _):
        greet(1 - z_odd, (2 * (index // 4) + side) * 4 + index % 4)
        return 0

    lax.fori_loop(0, 32, greet_all, 0)
    lax.fori_loop(0, 16, greet_some, 0)

    for copy in table_loads:
        copy.start()

    def load_own(step, _):
        tile = columns(step_tile(step, side))
        pltpu.make_async_copy(
            gas_hbm.at[:, tile], gas_own.at[step, pl.ds(0, GAS_ROWS)], own_sem.at[step]
        ).start()
        pltpu.make_async_copy(
            mass_hbm.at[:, tile], gas_own.at[step, pl.ds(GAS_ROWS, LEVELS)], own_sem.at[step]
        ).start()
        return 0

    lax.fori_loop(0, STEPS, load_own, 0)

    low_packed = lax.broadcasted_iota(jnp.int32, (PACKED_ROWS, LANES), 1) < HALF
    low8 = lax.broadcasted_iota(jnp.int32, (8, LANES), 1) < HALF

    for copy in state_loads:
        copy.wait()

    def sent_tile(step, z_low):
        z_to = 2 * ((z_block + 4 - step // 2) % 4) + z_low
        return 2 * z_to + (y_pair + step % 2) % 2

    def pack_step(step, _):
        for z_low in range(2):
            tile = sent_tile(step, z_low)
            row = pl.ds(tile, 1)
            kind = kind_ref[row, :]
            share = jnp.where(kind >= 1, cover_ref[row, :], 0.0)
            first = jnp.concatenate(
                [
                    cloud_ref[0:LEVELS, columns(tile)], kind.astype(F32), share,
                    age_ref[row, :], cosine_ref[row, :], jnp.zeros((4, LANES), F32),
                ],
                0,
            )
            second = jnp.concatenate(
                [
                    cloud_ref[LEVELS:CLOUD_ROWS, columns(tile)], lit_ref[row, :].astype(F32),
                    jnp.zeros((7, LANES), F32),
                ],
                0,
            )
            send[2 * tile] = jnp.where(low_packed, first, pltpu.roll(second, HALF, 1))
            send[2 * tile + 1] = jnp.where(low_packed, pltpu.roll(first, HALF, 1), second)
        return 0

    lax.fori_loop(0, AHEAD, pack_step, 0)

    pl.semaphore_wait(barrier, 48 - jnp.where(some_local, 1, 0))

    sent = pl.ds(0, SENT_ROWS)

    def send_step(step, _):
        tile = columns(step_tile(step, other))
        for source, target in (
            (gas_hbm.at[:, tile], gas_in.at[step, pl.ds(0, GAS_ROWS)]),
            (mass_hbm.at[:, tile], gas_in.at[step, pl.ds(GAS_ROWS, LEVELS)]),
        ):
            pltpu.make_async_remote_copy(
                src_ref=source, dst_ref=target, send_sem=gas_send, recv_sem=gas_recv.at[step],
                device_id=partner, device_id_type=MESH,
            ).start()
        for z_low in range(2):
            for low in range(2):
                k = 2 * sent_tile(step, z_low) + low
                here = jnp.logical_and(some_local, k == elem)
                source, target = send.at[k, sent], recv.at[step, side, y_low, sent]

                @pl.when(jnp.logical_not(here))
                def _():
                    pltpu.make_async_remote_copy(
                        src_ref=source, dst_ref=target, send_sem=state_send, recv_sem=state_recv.at[step],
                        device_id=device(z_odd, k), device_id_type=MESH,
                    ).start()

                @pl.when(here)
                def _():
                    pltpu.make_async_copy(source, target, state_recv.at[step]).start()

        return 0

    lax.fori_loop(0, AHEAD, send_step, 0)
    lax.fori_loop(AHEAD, STEPS, pack_step, 0)
    for copy in table_loads:
        copy.wait()
    make_tables(
        coeff_ref[...], ray_ref[...], cext_ref[...], weight_ref[...], surface_ref[...], snow_ref[...],
        coef_ref, solar_ref, albtab_ref,
    )
    x_ref[pl.ds(10 * LEVELS, 6 * LEVELS), :] = jnp.zeros((6 * LEVELS, LANES), F32)

    def one_tile(step, _):
        tile = step_tile(step, side)
        wait_bytes(gas_own.at[step], own_sem.at[step])
        wait_bytes(recv.at[step, :, :, sent], state_recv.at[step])
        wait_bytes(gas_in.at[step], gas_recv.at[step])

        @pl.when(step + AHEAD < STEPS)
        def _():
            send_step(step + AHEAD, 0)

        own0, own1 = recv[step, side, 0], recv[step, side, 1]
        other0, other1 = recv[step, other, 0], recv[step, other, 1]

        def lit_masks(block0, block1):
            row0, row1 = block0[LEVELS:], block1[LEVELS:]
            turned0, turned1 = pltpu.roll(row0, HALF, 1), pltpu.roll(row1, HALF, 1)
            return (
                jnp.where(low8, turned0, row0)[0:1] > 0.5,
                jnp.where(low8, turned1, row1)[0:1] > 0.5,
                jnp.where(low8, turned0, row1)[0:1] > 0.5,
            )

        mask0, mask1, own_lit = lit_masks(own0, own1)
        other_lit = lit_masks(other0, other1)[2]
        part0 = jnp.where(mask0, own0, other0)
        part1 = jnp.where(mask1, own1, other1)
        first = jnp.where(low_packed, part0, pltpu.roll(part1, HALF, 1))
        second = jnp.where(low_packed, pltpu.roll(part0, HALF, 1), part1)
        x_ref[pl.ds(0, FIELD_ROWS), :] = jnp.where(own_lit, gas_own[step], gas_in[step])
        x_ref[pl.ds(FIELD_ROWS, LEVELS), :] = first[0:LEVELS]
        x_ref[pl.ds(FIELD_ROWS + LEVELS, LEVELS), :] = second[0:LEVELS]
        heat, flux = compute_tile(
            x_ref, first[LEVELS:], coef_ref, solar_ref, albtab_ref, alb_ref, layer_ref, net_ref
        )
        for which_side in range(2):
            lit = jnp.where(which_side == side, own_lit.astype(F32), other_lit.astype(F32)) > 0.5
            kept = jnp.broadcast_to(jnp.where(lit, flux, 0.0), (8, LANES))
            flux_out[step, which_side, 0] = kept[0:1]
            flux_out[step, which_side, 1] = pltpu.roll(kept, HALF, 1)[0:1]
        for which_side in range(2):
            for low in range(2):
                k = 2 * tile + low
                here = jnp.logical_and(which_side == side, k == elem)
                source, target = flux_out.at[step, which_side, (low + y_low) % 2], flux_in.at[elem]

                @pl.when(jnp.logical_not(here))
                def _():
                    pltpu.make_async_remote_copy(
                        src_ref=source, dst_ref=target, send_sem=flux_send, recv_sem=flux_recv,
                        device_id=device(which_side, k), device_id_type=MESH,
                    ).start()

                @pl.when(here)
                def _():
                    pltpu.make_async_copy(source, target, flux_recv).start()

        heat_out[step] = jnp.where(other_lit, heat, 0.0)
        pltpu.make_async_remote_copy(
            src_ref=heat_out.at[step], dst_ref=heat_ref.at[:, columns(tile)],
            send_sem=heat_send, recv_sem=heat_recv,
            device_id=partner, device_id_type=MESH,
        ).start()
        heat_ref[:, columns(tile)] = jnp.where(own_lit, heat, 0.0)
        return 0

    lax.fori_loop(0, STEPS, one_tile, 0)

    wait_bytes(gas_in, gas_send)

    @pl.when(some_local)
    def _():
        wait_bytes(send.at[pl.ds(0, 31), sent], state_send)
        wait_bytes(flux_in.at[pl.ds(0, 31)], flux_send)

    @pl.when(jnp.logical_not(some_local))
    def _():
        wait_bytes(send.at[:, sent], state_send)
        wait_bytes(flux_in, flux_send)

    wait_bytes(heat_out, heat_send)
    wait_bytes(flux_in, flux_recv)
    for tile in range(TILES):
        flux_ref[tile : tile + 1, :] = jnp.where(low8[0:1], flux_in[2 * tile], flux_in[2 * tile + 1])
    wait_bytes(heat_out, heat_recv)


def body(
    gas_amounts, layer_mass, cloud_paths, surface_kind, snow_cover, snow_age, cos_zenith, sunlit,
    gas_coeff, rayleigh, cloud_ext, surface_table, snow_table, solar_weight,
):
    width = layer_mass.shape[1]
    rows = lambda x: x.reshape(width // LANES, LANES)
    dma = pltpu.SemaphoreType.DMA
    hbm = pl.BlockSpec(memory_space=SPACE)
    vmem = pl.BlockSpec(memory_space=pltpu.VMEM)
    wide = lambda *lead: pltpu.VMEM(lead + (LANES,), F32)
    heating, flux = pl.pallas_call(
        kernel,
        out_shape=(
            jax.ShapeDtypeStruct((LEVELS, width), F32),
            jax.ShapeDtypeStruct((width // LANES, LANES), F32),
        ),
        in_specs=[hbm] * 14,
        out_specs=(vmem, vmem),
        scratch_shapes=[
            wide(STEPS, FIELD_ROWS), pltpu.VMEM((CLOUD_ROWS, width), F32),
            pltpu.VMEM((TILES, LANES), jnp.int32), wide(TILES), wide(TILES), wide(TILES),
            pltpu.VMEM((TILES, LANES), jnp.int32),
            pltpu.VMEM((GASES, GPTS), F32), pltpu.VMEM((1, GPTS), F32), pltpu.VMEM((2, BANDS), F32),
            pltpu.VMEM((4, BANDS), F32), pltpu.VMEM((1, BANDS), F32), pltpu.VMEM((1, GPTS), F32),
            wide(STEPS, FIELD_ROWS), wide(32, PACKED_ROWS), wide(STEPS, 2, 2, PACKED_ROWS),
            wide(STEPS, LEVELS), wide(STEPS, 2, 2, 1), wide(32, 1),
            wide(16 * LEVELS), pltpu.VMEM((3 * GPTS, LANES), BF16), wide(GPTS), wide(80), wide(16),
            wide(LEVELS, 5, BANDS, 8), wide(LEVELS + 1, 8),
            dma((12,)), dma((STEPS,)), dma, dma((STEPS,)),
            dma, dma((STEPS,)), dma, dma, dma, dma,
        ],
        compiler_params=pltpu.CompilerParams(
            collective_id=0, has_side_effects=True, vmem_limit_bytes=60 * 2**20
        ),
    )(
        gas_amounts.reshape(GASES * LEVELS, width),
        layer_mass,
        cloud_paths.reshape(CLOUD_ROWS, width),
        rows(surface_kind), rows(snow_cover), rows(snow_age), rows(cos_zenith), rows(sunlit),
        gas_coeff, rayleigh.reshape(1, GPTS), cloud_ext, surface_table,
        snow_table.reshape(1, BANDS), solar_weight.reshape(1, GPTS),
    )
    return heating, flux.reshape(width)


def solution(mesh):
    columns = ("pair", "elem")
    placed = (
        P(None, None, columns), P(None, columns), P(None, None, columns),
        P(columns), P(columns), P(columns), P(columns), P(columns),
        P(), P(), P(), P(), P(), P(),
    )
    return jax.shard_map(
        body,
        mesh=mesh,
        in_specs=placed,
        out_specs=(P(None, columns), P(columns)),
        check_vma=False,
    )
```

time: 55.1 us -> 51.3 us (0.931)
  the two profiles are of different devices: /device:TPU:6 before, /device:TPU:32 now
where the time goes in v3:
time: 51.3 us; the launch traced here: 51.2 us
  Pallas kernels  47.6 us (93%)
  local copies, waits for them, and re-layouts  2.91 us (6%)
  between operations  0.64 us (1%)
    pallas_call x1, Pallas kernels, body(): pl.pallas_call(kernel, out_shape=(jax.ShapeDtypeStruct((LEVELS, width), F...  47.6 us
    unnamed x2, local copies, waits for them, and re-layouts  2.91 us

profile of v3, /device:TPU:32, one launch (start us, length us, event | category | flops | bytes accessed | tf_op | source)
XLA Modules:
  0.0 51.2 jit_solution(7894301321553073484)
XLA Ops:
  0.6 47.6 %shard_map.149 = (f32[24,2048]{1,0:T(8,128)}, f32[16,128]{1,0:T(8,128)}) custom-call(f32[168,2048]{1,0:T(8,128)} %bitcast.11, f32[24,2048]{1,0:T(8,128)} %mass_hbm.1, f32[48,2048]{1,0:T(8,128)} %bitcast.12, s32[16,128]{1,0:T(8,128)} %bitcast.13, f32[16,128]{1,0:T(8,128)} %bitcast.14, f32[16,128]{1,0:T(8,128)} %bitcast.15, f32[16,128]{1,0:T(8,128)} %bitcast.16, ...), custom_call_target="tpu_custom_call" | custom-call | tf_op jit(solution)/shard_map/pallas_call | solution.py:408
  48.3 1.6 %copy.18 = f32[24,2048]{1,0:T(8,128)} copy(f32[24,2048]{1,0:T(8,128)} %get-tuple-element.8) | data formatting | bytes 393216
  49.9 1.3 %copy.19 = f32[2048]{0:T(1024)} copy(f32[2048]{0:T(1024)} %bitcast.18) | data formatting | bytes 16384

commit v4 on v3

--- a/solution.py
+++ b/solution.py
@@ -29,6 +29,7 @@
 SENT_ROWS = 28
 AHEAD = 3
 STEPS = 8
+TURNS = STEPS + 1
 TILES = 16
 UNROLL = 24
 MESH = pl.DeviceIdType.MESH
@@ -89,8 +90,9 @@
         alb, src = carried
         layer = LEVELS - 1 - step
         x1, x2, x3 = split3(x_ref[pl.ds(layer, 16, stride=LEVELS), :])
-        terms = jnp.concatenate([x1, x2, x1, x3, x1, x2, jnp.zeros((32, LANES), F32)], 0)
-        optics = jnp.dot(coef_ref[...], terms.astype(BF16), preferred_element_type=F32)
+        x1, x2, x3 = (part.astype(BF16) for part in (x1, x2, x3))
+        terms = jnp.concatenate([x1, x2, x1, x3, x1, x2, jnp.zeros((32, LANES), BF16)], 0)
+        optics = jnp.dot(coef_ref[...], terms, preferred_element_type=F32)
         next_alb, next_src = [], []
         for b in range(BANDS):
             depth = optics[8 * b : 8 * b + 8]
@@ -151,9 +153,9 @@
     gas_hbm, mass_hbm, cloud_hbm, kind_hbm, cover_hbm, age_hbm, cosine_hbm, lit_hbm,
     coeff_hbm, ray_hbm, cext_hbm, surface_hbm, snow_hbm, weight_hbm,
     heat_ref, flux_ref,
-    gas_own, cloud_ref, kind_ref, cover_ref, age_ref, cosine_ref, lit_ref,
+    gases, cloud_ref, kind_ref, cover_ref, age_ref, cosine_ref, lit_ref,
     coeff_ref, ray_ref, cext_ref, surface_ref, snow_ref, weight_ref,
-    gas_in, send, recv, heat_out, flux_out, flux_in,
+    send, recv, heat_out, flux_out, flux_in,
     x_ref, coef_ref, solar_ref, albtab_ref, alb_ref, layer_ref, net_ref,
     load_sem, own_sem, gas_send, gas_recv,
     state_send, state_recv, heat_send, heat_recv, flux_send, flux_recv,
@@ -164,7 +166,6 @@
     z, y = elem // 4, elem % 4
     z_block, z_odd, y_pair, y_low = z // 2, z % 2, y // 2, y % 2
     other = 1 - side
-    some_local = z_odd == side
 
     def device(which_side, which_elem):
         return (which_side * half_pairs + group, which_elem)
@@ -179,6 +180,10 @@
 
     def step_tile(step, which_side):
         return 2 * (2 * ((z_block + step // 2) % 4) + which_side) + (y_pair + step % 2) % 2
+
+    def sent_tile(step, z_low):
+        z_to = 2 * ((z_block + 4 - step // 2) % 4) + z_low
+        return 2 * z_to + (y_pair + step % 2) % 2
 
     state_loads = [
         pltpu.make_async_copy(source, target, load_sem.at[index])
@@ -200,45 +205,49 @@
     barrier = pltpu.get_barrier_semaphore()
 
     def greet(which_side, k):
-        @pl.when(jnp.logical_or(which_side != side, k != elem))
-        def _():
-            pl.semaphore_signal(barrier, inc=1, device_id=device(which_side, k), device_id_type=MESH)
-
-    def greet_all(k, _):
-        greet(z_odd, k)
+        pl.semaphore_signal(barrier, inc=1, device_id=device(which_side, k), device_id_type=MESH)
+
+    greet(other, elem)
+
+    def greet_step(step, _):
+        for low in range(2):
+            for z_low in range(2):
+                greet(z_odd, 2 * sent_tile(step, z_low) + low)
+            greet(1 - z_odd, 2 * step_tile(step, side) + low)
         return 0
 
-    def greet_some(index, _):
-        greet(1 - z_odd, (2 * (index // 4) + side) * 4 + index % 4)
-        return 0
-
-    lax.fori_loop(0, 32, greet_all, 0)
-    lax.fori_loop(0, 16, greet_some, 0)
+    lax.fori_loop(1, STEPS, greet_step, 0)
+    for z_low in range(2):
+        for low in range(2):
+            near = 2 * sent_tile(0, z_low) + low
+
+            @pl.when(near != elem)
+            def _():
+                greet(side, near)
 
     for copy in table_loads:
         copy.start()
 
-    def load_own(step, _):
-        tile = columns(step_tile(step, side))
+    def turn_tile(turn):
+        return step_tile(turn % STEPS, jnp.where(turn == STEPS, other, side))
+
+    def load_own(turn, _):
+        tile = columns(turn_tile(turn))
         pltpu.make_async_copy(
-            gas_hbm.at[:, tile], gas_own.at[step, pl.ds(0, GAS_ROWS)], own_sem.at[step]
+            gas_hbm.at[:, tile], gases.at[turn, pl.ds(0, GAS_ROWS)], own_sem.at[turn]
         ).start()
         pltpu.make_async_copy(
-            mass_hbm.at[:, tile], gas_own.at[step, pl.ds(GAS_ROWS, LEVELS)], own_sem.at[step]
+            mass_hbm.at[:, tile], gases.at[turn, pl.ds(GAS_ROWS, LEVELS)], own_sem.at[turn]
         ).start()
         return 0
 
-    lax.fori_loop(0, STEPS, load_own, 0)
+    lax.fori_loop(0, TURNS, load_own, 0)
 
     low_packed = lax.broadcasted_iota(jnp.int32, (PACKED_ROWS, LANES), 1) < HALF
     low8 = lax.broadcasted_iota(jnp.int32, (8, LANES), 1) < HALF
 
     for copy in state_loads:
         copy.wait()
-
-    def sent_tile(step, z_low):
-        z_to = 2 * ((z_block + 4 - step // 2) % 4) + z_low
-        return 2 * z_to + (y_pair + step % 2) % 2
 
     def pack_step(step, _):
         for z_low in range(2):
@@ -266,15 +275,33 @@
 
     lax.fori_loop(0, AHEAD, pack_step, 0)
 
-    pl.semaphore_wait(barrier, 48 - jnp.where(some_local, 1, 0))
+    pl.semaphore_wait(barrier, 46)
 
     sent = pl.ds(0, SENT_ROWS)
+
+    def send_near():
+        for z_low in range(2):
+            for low in range(2):
+                k = 2 * sent_tile(0, z_low) + low
+                source, target = send.at[k, sent], recv.at[0, z_odd, y_low, sent]
+
+                @pl.when(k != elem)
+                def _():
+                    pltpu.make_async_remote_copy(
+                        src_ref=source, dst_ref=target, send_sem=state_send, recv_sem=state_recv.at[0],
+                        device_id=device(side, k), device_id_type=MESH,
+                    ).start()
+
+                @pl.when(k == elem)
+                def _():
+                    pltpu.make_async_copy(source, target, state_recv.at[0]).start()
 
     def send_step(step, _):
         tile = columns(step_tile(step, other))
+        slot = STEPS + step
         for source, target in (
-            (gas_hbm.at[:, tile], gas_in.at[step, pl.ds(0, GAS_ROWS)]),
-            (mass_hbm.at[:, tile], gas_in.at[step, pl.ds(GAS_ROWS, LEVELS)]),
+            (gas_hbm.at[:, tile], gases.at[slot, pl.ds(0, GAS_ROWS)]),
+            (mass_hbm.at[:, tile], gases.at[slot, pl.ds(GAS_ROWS, LEVELS)]),
         ):
             pltpu.make_async_remote_copy(
                 src_ref=source, dst_ref=target, send_sem=gas_send, recv_sem=gas_recv.at[step],
@@ -283,23 +310,15 @@
         for z_low in range(2):
             for low in range(2):
                 k = 2 * sent_tile(step, z_low) + low
-                here = jnp.logical_and(some_local, k == elem)
-                source, target = send.at[k, sent], recv.at[step, side, y_low, sent]
-
-                @pl.when(jnp.logical_not(here))
-                def _():
-                    pltpu.make_async_remote_copy(
-                        src_ref=source, dst_ref=target, send_sem=state_send, recv_sem=state_recv.at[step],
-                        device_id=device(z_odd, k), device_id_type=MESH,
-                    ).start()
-
-                @pl.when(here)
-                def _():
-                    pltpu.make_async_copy(source, target, state_recv.at[step]).start()
-
+                pltpu.make_async_remote_copy(
+                    src_ref=send.at[k, sent], dst_ref=recv.at[step, side, y_low, sent],
+                    send_sem=state_send, recv_sem=state_recv.at[step],
+                    device_id=device(z_odd, k), device_id_type=MESH,
+                ).start()
         return 0
 
-    lax.fori_loop(0, AHEAD, send_step, 0)
+    send_near()
+    lax.fori_loop(1, AHEAD, send_step, 0)
     lax.fori_loop(AHEAD, STEPS, pack_step, 0)
     for copy in table_loads:
         copy.wait()
@@ -309,18 +328,29 @@
     )
     x_ref[pl.ds(10 * LEVELS, 6 * LEVELS), :] = jnp.zeros((6 * LEVELS, LANES), F32)
 
-    def one_tile(step, _):
-        tile = step_tile(step, side)
-        wait_bytes(gas_own.at[step], own_sem.at[step])
-        wait_bytes(recv.at[step, :, :, sent], state_recv.at[step])
-        wait_bytes(gas_in.at[step], gas_recv.at[step])
-
-        @pl.when(step + AHEAD < STEPS)
+    def one_tile(turn, _):
+        last = turn == STEPS
+        step = turn % STEPS
+        tile = turn_tile(turn)
+        alone = step == 0
+        wait_bytes(gases.at[turn], own_sem.at[turn])
+
+        @pl.when(jnp.logical_not(last))
         def _():
-            send_step(step + AHEAD, 0)
-
-        own0, own1 = recv[step, side, 0], recv[step, side, 1]
-        other0, other1 = recv[step, other, 0], recv[step, other, 1]
+            wait_bytes(recv.at[step, :, :, sent], state_recv.at[step])
+
+        @pl.when(jnp.logical_not(alone))
+        def _():
+            wait_bytes(gases.at[STEPS + step], gas_recv.at[step])
+
+        @pl.when(turn + AHEAD < STEPS)
+        def _():
+            send_step(turn + AHEAD, 0)
+
+        mine = jnp.where(last, other, side)
+        theirs = jnp.where(alone, mine, other)
+        own0, own1 = recv[step, mine, 0], recv[step, mine, 1]
+        other0, other1 = recv[step, theirs, 0], recv[step, theirs, 1]
 
         def lit_masks(block0, block1):
             row0, row1 = block0[LEVELS:], block1[LEVELS:]
@@ -337,7 +367,9 @@
         part1 = jnp.where(mask1, own1, other1)
         first = jnp.where(low_packed, part0, pltpu.roll(part1, HALF, 1))
         second = jnp.where(low_packed, pltpu.roll(part0, HALF, 1), part1)
-        x_ref[pl.ds(0, FIELD_ROWS), :] = jnp.where(own_lit, gas_own[step], gas_in[step])
+        x_ref[pl.ds(0, FIELD_ROWS), :] = jnp.where(
+            own_lit, gases[turn], gases[jnp.where(alone, turn, STEPS + step)]
+        )
         x_ref[pl.ds(FIELD_ROWS, LEVELS), :] = first[0:LEVELS]
         x_ref[pl.ds(FIELD_ROWS + LEVELS, LEVELS), :] = second[0:LEVELS]
         heat, flux = compute_tile(
@@ -346,15 +378,16 @@
         for which_side in range(2):
             lit = jnp.where(which_side == side, own_lit.astype(F32), other_lit.astype(F32)) > 0.5
             kept = jnp.broadcast_to(jnp.where(lit, flux, 0.0), (8, LANES))
-            flux_out[step, which_side, 0] = kept[0:1]
-            flux_out[step, which_side, 1] = pltpu.roll(kept, HALF, 1)[0:1]
+            flux_out[turn, which_side, 0] = kept[0:1]
+            flux_out[turn, which_side, 1] = pltpu.roll(kept, HALF, 1)[0:1]
         for which_side in range(2):
             for low in range(2):
                 k = 2 * tile + low
                 here = jnp.logical_and(which_side == side, k == elem)
-                source, target = flux_out.at[step, which_side, (low + y_low) % 2], flux_in.at[elem]
-
-                @pl.when(jnp.logical_not(here))
+                wanted = jnp.logical_or(which_side == side, jnp.logical_not(alone))
+                source, target = flux_out.at[turn, which_side, (low + y_low) % 2], flux_in.at[elem]
+
+                @pl.when(jnp.logical_and(wanted, jnp.logical_not(here)))
                 def _():
                     pltpu.make_async_remote_copy(
                         src_ref=source, dst_ref=target, send_sem=flux_send, recv_sem=flux_recv,
@@ -365,29 +398,23 @@
                 def _():
                     pltpu.make_async_copy(source, target, flux_recv).start()
 
-        heat_out[step] = jnp.where(other_lit, heat, 0.0)
-        pltpu.make_async_remote_copy(
-            src_ref=heat_out.at[step], dst_ref=heat_ref.at[:, columns(tile)],
-            send_sem=heat_send, recv_sem=heat_recv,
-            device_id=partner, device_id_type=MESH,
-        ).start()
+        @pl.when(jnp.logical_not(alone))
+        def _():
+            heat_out[step - 1] = jnp.where(other_lit, heat, 0.0)
+            pltpu.make_async_remote_copy(
+                src_ref=heat_out.at[step - 1], dst_ref=heat_ref.at[:, columns(tile)],
+                send_sem=heat_send, recv_sem=heat_recv,
+                device_id=partner, device_id_type=MESH,
+            ).start()
+
         heat_ref[:, columns(tile)] = jnp.where(own_lit, heat, 0.0)
         return 0
 
-    lax.fori_loop(0, STEPS, one_tile, 0)
-
-    wait_bytes(gas_in, gas_send)
-
-    @pl.when(some_local)
-    def _():
-        wait_bytes(send.at[pl.ds(0, 31), sent], state_send)
-        wait_bytes(flux_in.at[pl.ds(0, 31)], flux_send)
-
-    @pl.when(jnp.logical_not(some_local))
-    def _():
-        wait_bytes(send.at[:, sent], state_send)
-        wait_bytes(flux_in, flux_send)
-
+    lax.fori_loop(0, TURNS, one_tile, 0)
+
+    wait_bytes(gases.at[pl.ds(TURNS, STEPS - 1)], gas_send)
+    wait_bytes(send.at[pl.ds(0, 31), sent], state_send)
+    wait_bytes(flux_in.at[pl.ds(0, 31)], flux_send)
     wait_bytes(heat_out, heat_send)
     wait_bytes(flux_in, flux_recv)
     for tile in range(TILES):
@@ -414,16 +441,16 @@
         in_specs=[hbm] * 14,
         out_specs=(vmem, vmem),
         scratch_shapes=[
-            wide(STEPS, FIELD_ROWS), pltpu.VMEM((CLOUD_ROWS, width), F32),
+            wide(2 * STEPS, FIELD_ROWS), pltpu.VMEM((CLOUD_ROWS, width), F32),
             pltpu.VMEM((TILES, LANES), jnp.int32), wide(TILES), wide(TILES), wide(TILES),
             pltpu.VMEM((TILES, LANES), jnp.int32),
             pltpu.VMEM((GASES, GPTS), F32), pltpu.VMEM((1, GPTS), F32), pltpu.VMEM((2, BANDS), F32),
             pltpu.VMEM((4, BANDS), F32), pltpu.VMEM((1, BANDS), F32), pltpu.VMEM((1, GPTS), F32),
-            wide(STEPS, FIELD_ROWS), wide(32, PACKED_ROWS), wide(STEPS, 2, 2, PACKED_ROWS),
-            wide(STEPS, LEVELS), wide(STEPS, 2, 2, 1), wide(32, 1),
+            wide(32, PACKED_ROWS), wide(STEPS, 2, 2, PACKED_ROWS),
+            wide(STEPS - 1, LEVELS), wide(TURNS, 2, 2, 1), wide(32, 1),
             wide(16 * LEVELS), pltpu.VMEM((3 * GPTS, LANES), BF16), wide(GPTS), wide(80), wide(16),
             wide(LEVELS, 5, BANDS, 8), wide(LEVELS + 1, 8),
-            dma((12,)), dma((STEPS,)), dma, dma((STEPS,)),
+            dma((12,)), dma((TURNS,)), dma, dma((STEPS,)),
             dma, dma((STEPS,)), dma, dma, dma, dma,
         ],
         compiler_params=pltpu.CompilerParams(

time: 51.3 us -> 48 us (0.936)
  the two profiles are of different devices: /device:TPU:32 before, /device:TPU:6 now
where the time goes in v4:
time: 48 us; the launch traced here: 47.3 us
  Pallas kernels  43.8 us (91%)
  local copies, waits for them, and re-layouts  2.91 us (6%)
  between operations  0.64 us (1%)
    pallas_call x1, Pallas kernels, body(): pl.pallas_call(kernel, out_shape=(jax.ShapeDtypeStruct((LEVELS, width), F...  43.8 us
    unnamed x2, local copies, waits for them, and re-layouts  2.91 us

profile of v4, /device:TPU:6, one launch (start us, length us, event | category | flops | bytes accessed | tf_op | source)
XLA Modules:
  0.0 47.3 jit_solution(16913677489655115695)
XLA Ops:
  0.6 43.8 %shard_map.149 = (f32[24,2048]{1,0:T(8,128)}, f32[16,128]{1,0:T(8,128)}) custom-call(f32[168,2048]{1,0:T(8,128)} %bitcast.11, f32[24,2048]{1,0:T(8,128)} %mass_hbm.1, f32[48,2048]{1,0:T(8,128)} %bitcast.12, s32[16,128]{1,0:T(8,128)} %bitcast.13, f32[16,128]{1,0:T(8,128)} %bitcast.14, f32[16,128]{1,0:T(8,128)} %bitcast.15, f32[16,128]{1,0:T(8,128)} %bitcast.16, ...), custom_call_target="tpu_custom_call" | custom-call | tf_op jit(solution)/shard_map/pallas_call | solution.py:435
  44.4 1.6 %copy.18 = f32[24,2048]{1,0:T(8,128)} copy(f32[24,2048]{1,0:T(8,128)} %get-tuple-element.8) | data formatting | bytes 393216
  46.0 1.3 %copy.19 = f32[2048]{0:T(1024)} copy(f32[2048]{0:T(1024)} %bitcast.18) | data formatting | bytes 16384

commit v5 on v4

--- a/solution.py
+++ b/solution.py
@@ -97,12 +97,12 @@
         for b in range(BANDS):
             depth = optics[8 * b : 8 * b + 8]
             inv_depth = pl.reciprocal(depth, approx=True)
-            backward = optics[GPTS + 8 * b : GPTS + 8 * b + 8] * inv_depth
-            onward = optics[2 * GPTS + 8 * b : 2 * GPTS + 8 * b + 8] * inv_depth
+            backward = optics[GPTS + 8 * b : GPTS + 8 * b + 8]
+            onward = optics[2 * GPTS + 8 * b : 2 * GPTS + 8 * b + 8]
             diffuse_exp = jnp.exp2(depth)
             beam_exp = jnp.exp2(depth * beam_scale)
-            diffuse_loss = 1.0 - diffuse_exp
-            beam_loss = 1.0 - beam_exp
+            diffuse_loss = (1.0 - diffuse_exp) * inv_depth
+            beam_loss = (1.0 - beam_exp) * inv_depth
             refl_diff = backward * diffuse_loss
             tran_diff = diffuse_exp + onward * diffuse_loss
             refl_dir = backward * beam_loss
@@ -127,19 +127,18 @@
 
     def downward(layer, carried):
         down, direct = carried
-        nets, next_down, next_direct = [], [], []
+        net = jnp.zeros(block, F32)
+        next_down, next_direct = [], []
         for b in range(BANDS):
-            nets.append(layer_ref[layer, 3, b] * down[b] + layer_ref[layer, 4, b] * direct[b])
+            net = net + (layer_ref[layer, 3, b] * down[b] + layer_ref[layer, 4, b] * direct[b])
             next_down.append(layer_ref[layer, 0, b] * down[b] + layer_ref[layer, 1, b] * direct[b])
             next_direct.append(layer_ref[layer, 2, b] * direct[b])
-        while len(nets) > 1:
-            nets = [sum(nets[i : i + 2][1:], nets[i]) for i in range(0, len(nets), 2)]
-        net_ref[layer] = nets[0]
+        net_ref[layer] = net
         return tuple(next_down), tuple(next_direct)
 
     beam = tuple(solar_ref[pl.ds(8 * b, 8), :] * cosine for b in range(BANDS))
     none = tuple(jnp.zeros(block, F32) for b in range(BANDS))
-    down, direct = lax.fori_loop(0, LEVELS, downward, (none, beam), unroll=UNROLL)
+    down, direct = lax.fori_loop(0, LEVELS, downward, (none, beam), unroll=UNROLL // 2)
     net = jnp.zeros(block, F32)
     for b in range(BANDS):
         net = net + (1.0 - jnp.broadcast_to(alb_ref[b : b + 1, :], block)) * (down[b] + direct[b])
@@ -199,8 +198,6 @@
             (surface_hbm, surface_ref), (snow_hbm, snow_ref), (weight_hbm, weight_ref),
         ))
     ]
-    for copy in state_loads:
-        copy.start()
 
     barrier = pltpu.get_barrier_semaphore()
 
@@ -225,6 +222,8 @@
             def _():
                 greet(side, near)
 
+    for copy in state_loads:
+        copy.start()
     for copy in table_loads:
         copy.start()
 
@@ -241,7 +240,7 @@
         ).start()
         return 0
 
-    lax.fori_loop(0, TURNS, load_own, 0)
+    load_own(0, 0)
 
     low_packed = lax.broadcasted_iota(jnp.int32, (PACKED_ROWS, LANES), 1) < HALF
     low8 = lax.broadcasted_iota(jnp.int32, (8, LANES), 1) < HALF
@@ -273,7 +272,7 @@
             send[2 * tile + 1] = jnp.where(low_packed, pltpu.roll(first, HALF, 1), second)
         return 0
 
-    lax.fori_loop(0, AHEAD, pack_step, 0)
+    pack_step(0, 0)
 
     pl.semaphore_wait(barrier, 46)
 
@@ -318,7 +317,13 @@
         return 0
 
     send_near()
-    lax.fori_loop(1, AHEAD, send_step, 0)
+
+    def pack_and_send(step, _):
+        pack_step(step, 0)
+        return send_step(step, 0)
+
+    lax.fori_loop(1, AHEAD, pack_and_send, 0)
+    lax.fori_loop(1, TURNS, load_own, 0)
     lax.fori_loop(AHEAD, STEPS, pack_step, 0)
     for copy in table_loads:
         copy.wait()
@@ -380,23 +385,27 @@
             kept = jnp.broadcast_to(jnp.where(lit, flux, 0.0), (8, LANES))
             flux_out[turn, which_side, 0] = kept[0:1]
             flux_out[turn, which_side, 1] = pltpu.roll(kept, HALF, 1)[0:1]
-        for which_side in range(2):
+        def flux_copy(which_side, low):
+            return pltpu.make_async_remote_copy(
+                src_ref=flux_out.at[turn, which_side, (low + y_low) % 2], dst_ref=flux_in.at[elem],
+                send_sem=flux_send, recv_sem=flux_recv,
+                device_id=device(which_side, 2 * tile + low), device_id_type=MESH,
+            )
+
+        @pl.when(alone)
+        def _():
             for low in range(2):
-                k = 2 * tile + low
-                here = jnp.logical_and(which_side == side, k == elem)
-                wanted = jnp.logical_or(which_side == side, jnp.logical_not(alone))
-                source, target = flux_out.at[turn, which_side, (low + y_low) % 2], flux_in.at[elem]
-
-                @pl.when(jnp.logical_and(wanted, jnp.logical_not(here)))
+                here = 2 * tile + low == elem
+
+                @pl.when(jnp.logical_not(here))
                 def _():
-                    pltpu.make_async_remote_copy(
-                        src_ref=source, dst_ref=target, send_sem=flux_send, recv_sem=flux_recv,
-                        device_id=device(which_side, k), device_id_type=MESH,
-                    ).start()
+                    flux_copy(side, low).start()
 
                 @pl.when(here)
                 def _():
-                    pltpu.make_async_copy(source, target, flux_recv).start()
+                    pltpu.make_async_copy(
+                        flux_out.at[turn, side, (low + y_low) % 2], flux_in.at[elem], flux_recv
+                    ).start()
 
         @pl.when(jnp.logical_not(alone))
         def _():
@@ -406,6 +415,9 @@
                 send_sem=heat_send, recv_sem=heat_recv,
                 device_id=partner, device_id_type=MESH,
             ).start()
+            for which_side in range(2):
+                for low in range(2):
+                    flux_copy(which_side, low).start()
 
         heat_ref[:, columns(tile)] = jnp.where(own_lit, heat, 0.0)
         return 0

time: 48 us -> 47.3 us (0.985)
  no operation moved by 1% of the time
where the time goes in v5:
time: 47.3 us; the launch traced here: 47.1 us
  Pallas kernels  43.5 us (92%)
  local copies, waits for them, and re-layouts  2.91 us (6%)
  between operations  0.64 us (1%)
    pallas_call x1, Pallas kernels, body(): pl.pallas_call(kernel, out_shape=(jax.ShapeDtypeStruct((LEVELS, width), F...  43.5 us
    unnamed x2, local copies, waits for them, and re-layouts  2.91 us

profile of v5, /device:TPU:6, one launch (start us, length us, event | category | flops | bytes accessed | tf_op | source)
XLA Modules:
  0.0 47.1 jit_solution(5519319112850799480)
XLA Ops:
  0.6 43.5 %shard_map.149 = (f32[24,2048]{1,0:T(8,128)}, f32[16,128]{1,0:T(8,128)}) custom-call(f32[168,2048]{1,0:T(8,128)} %bitcast.11, f32[24,2048]{1,0:T(8,128)} %mass_hbm.1, f32[48,2048]{1,0:T(8,128)} %bitcast.12, s32[16,128]{1,0:T(8,128)} %bitcast.13, f32[16,128]{1,0:T(8,128)} %bitcast.14, f32[16,128]{1,0:T(8,128)} %bitcast.15, f32[16,128]{1,0:T(8,128)} %bitcast.16, ...), custom_call_target="tpu_custom_call" | custom-call | tf_op jit(solution)/shard_map/pallas_call | solution.py:447
  44.2 1.6 %copy.18 = f32[24,2048]{1,0:T(8,128)} copy(f32[24,2048]{1,0:T(8,128)} %get-tuple-element.8) | data formatting | bytes 393216
  45.8 1.3 %copy.19 = f32[2048]{0:T(1024)} copy(f32[2048]{0:T(1024)} %bitcast.18) | data formatting | bytes 16384
